TPU v7x, 512 devices: a whole 4x4x16 slice. The times are simulated.
512 devices in a mesh: context: 128 (over z_lo, y, x, core), tensor: 4 (over z_hi).
Axes of the slice: x: 4, y: 4, z: 16 (z_hi: 4, z_lo: 4; z = z_hi * 4 + z_lo), core: 2. Of those that a mesh axis runs over, the one named last changes fastest.
Arguments:
- query_gate: bfloat16 [16384, 4096], P('context', 'tensor'), may hold values from -12 to 12
- key_branch: bfloat16 [16384, 4096], P('context', 'tensor'), may hold values from -6 to 6
- value_branch: bfloat16 [16384, 4096], P('context', 'tensor'), may hold values from -6 to 6
- filter_spectrum: float32 [128, 2, 2, 256, 128], P('context', None, None, 'tensor'), may hold values from -4 to 4, as said below
- norm_gain: bfloat16 [4096], P('tensor'), may hold values from 0.5 to 1.5
Outputs:
- gated_mix: float32 [16384, 4096], P('context', 'tensor')
- normed: bfloat16 [16384, 4096], P('context', 'tensor')
Inputs may be any that keep to these rules, and one draw needn't show every extreme that they name: `filter_spectrum`: every group's response is that of a real filter: response_g[32768 - k] is the complex conjugate of response_g[k] (indices modulo 32768).
All inputs are finite; a program needn't handle non-finite values.
Results may differ from a plain program's by a relative error of at most 0.001.
Values sent between devices are 32-bit elements; how exact they have to be, the bound alone decides.
A program may use at most 64 MiB of HBM per device.

v0:
```python
import math

import jax
import jax.numpy as jnp
from jax import lax
from jax.sharding import PartitionSpec as P

CHANNELS = 4096
GROUP = 16


HIGHEST = lax.Precision.HIGHEST
EPSILON = 1e-06


def swapped(value, axis, distance):
    return lax.ppermute(value, axis, [(i, i ^ 1 << distance) for i in range(lax.axis_size(axis))])


def split_pairs(block, group_size):
    tokens_here, channels_here = block.shape
    shaped = block.reshape(tokens_here, channels_here // group_size, 2, group_size // 2)
    real_part = shaped[:, :, 0, :].reshape(tokens_here, channels_here // 2)
    imag_part = shaped[:, :, 1, :].reshape(tokens_here, channels_here // 2)
    return (real_part, imag_part)


def join_pairs(real_part, imag_part, group_size):
    tokens_here, columns = real_part.shape
    stacked = jnp.stack(
        [
            real_part.reshape(tokens_here, -1, group_size // 2),
            imag_part.reshape(tokens_here, -1, group_size // 2),
        ],
        axis=2,
    )
    return stacked.reshape(tokens_here, columns * 2)


def complex_product(left_re, left_im, right_re, right_im):
    return (left_re * right_re - left_im * right_im, left_re * right_im + left_im * right_re)


def reversed_index(position, places):
    flipped = jnp.zeros((), jnp.int32)
    for shift_place in range(places):
        flipped = flipped + (position >> shift_place & 1) * (1 << places - 1 - shift_place)
    return flipped


def frequency_tables(starts, tokens_here, stride, freqs):
    steps_j = jnp.arange(tokens_here, dtype=jnp.int32)
    waves = starts[:, None] + stride * steps_j[None, :]
    phases = waves[:, :, None] * steps_j[None, None, :] % freqs
    angles = phases.astype(jnp.float32) * (-2.0 * math.pi / freqs)
    return (jnp.cos(angles), jnp.sin(angles))


def einsum_high(formula, left, right):
    return jnp.einsum(formula, left, right, precision=HIGHEST, preferred_element_type=jnp.float32)


def on_device(query_gate, key_branch, value_branch, filter_spectrum, norm_gain):
    sources = lax.axis_size("context")
    places = sources.bit_length() - 1
    position = lax.axis_index("context")
    tokens_here = key_branch.shape[0]
    freqs = 2 * tokens_here * sources
    driven = key_branch.astype(jnp.float32) * value_branch.astype(jnp.float32)
    signal_re, signal_im = split_pairs(driven, GROUP)
    flipped = reversed_index(position, places)
    starts = 2 * flipped + jnp.arange(2, dtype=jnp.int32)
    cos_table, sin_table = frequency_tables(starts, tokens_here, 2 * sources, freqs)
    rotation = position.astype(jnp.float32) * (-math.pi / sources)
    shifted_re, shifted_im = complex_product(
        signal_re, signal_im, jnp.cos(rotation), jnp.sin(rotation)
    )
    work_re = jnp.stack([signal_re, shifted_re])
    work_im = jnp.stack([signal_im, shifted_im])
    for section_num in range(places):
        section_bit = places - 1 - section_num
        half_span = 1 << section_bit
        other_re, other_im = swapped((work_re, work_im), "context", section_bit)
        upper_half = position >> section_bit & 1 == 1
        low_re = jnp.where(upper_half, other_re, work_re)
        low_im = jnp.where(upper_half, other_im, work_im)
        high_re = jnp.where(upper_half, work_re, other_re)
        high_im = jnp.where(upper_half, work_im, other_im)
        twist_angle = (position % half_span).astype(jnp.float32) * (-math.pi / half_span)
        diff_re, diff_im = complex_product(
            low_re - high_re, low_im - high_im, jnp.cos(twist_angle), jnp.sin(twist_angle)
        )
        work_re = jnp.where(upper_half, diff_re, low_re + high_re)
        work_im = jnp.where(upper_half, diff_im, low_im + high_im)
    columns_re, columns_im = (work_re, work_im)
    freq_re = einsum_high("cbj,cjq->cbq", cos_table, columns_re) - einsum_high(
        "cbj,cjq->cbq", sin_table, columns_im
    )
    freq_im = einsum_high("cbj,cjq->cbq", cos_table, columns_im) + einsum_high(
        "cbj,cjq->cbq", sin_table, columns_re
    )
    filter_re = jnp.repeat(jnp.transpose(filter_spectrum[0, 0], (0, 2, 1)), GROUP // 2, axis=2)
    filter_im = jnp.repeat(jnp.transpose(filter_spectrum[0, 1], (0, 2, 1)), GROUP // 2, axis=2)
    prod_re, prod_im = complex_product(freq_re, freq_im, filter_re, filter_im)
    inverse_re = einsum_high("cbj,cbq->cjq", cos_table, prod_re) + einsum_high(
        "cbj,cbq->cjq", sin_table, prod_im
    )
    inverse_im = einsum_high("cbj,cbq->cjq", cos_table, prod_im) - einsum_high(
        "cbj,cbq->cjq", sin_table, prod_re
    )
    for section_num in range(places):
        section_bit = section_num
        half_span = 1 << section_bit
        other_re, other_im = swapped((inverse_re, inverse_im), "context", section_bit)
        upper_half = position >> section_bit & 1 == 1
        low_re = jnp.where(upper_half, other_re, inverse_re)
        low_im = jnp.where(upper_half, other_im, inverse_im)
        high_re = jnp.where(upper_half, inverse_re, other_re)
        high_im = jnp.where(upper_half, inverse_im, other_im)
        twist_angle = (position % half_span).astype(jnp.float32) * (math.pi / half_span)
        turned_re, turned_im = complex_product(
            high_re, high_im, jnp.cos(twist_angle), jnp.sin(twist_angle)
        )
        inverse_re = jnp.where(upper_half, low_re - turned_re, low_re + turned_re)
        inverse_im = jnp.where(upper_half, low_im - turned_im, low_im + turned_im)
    rotation = position.astype(jnp.float32) * (math.pi / sources)
    extra_re, extra_im = complex_product(
        inverse_re[1], inverse_im[1], jnp.cos(rotation), jnp.sin(rotation)
    )
    time_re = (inverse_re[0] + extra_re) / freqs
    time_im = (inverse_im[0] + extra_im) / freqs
    convolved = join_pairs(time_re, time_im, GROUP)
    gated_mix = query_gate.astype(jnp.float32) * convolved
    squares = lax.psum(jnp.sum(gated_mix * gated_mix, axis=1), "tensor")
    mean_square = squares[:, None] / CHANNELS
    normed = (gated_mix * lax.rsqrt(mean_square + EPSILON) * norm_gain.astype(jnp.float32)).astype(
        jnp.bfloat16
    )
    return (gated_mix, normed)


def solution(mesh):
    placed = (
        P("context", "tensor"),
        P("context", "tensor"),
        P("context", "tensor"),
        P("context", None, None, "tensor", None),
        P("tensor"),
    )
    return jax.shard_map(
        on_device,
        mesh=mesh,
        in_specs=placed,
        out_specs=(P("context", "tensor"), P("context", "tensor")),
        check_vma=False,
    )
```

profile of v0, /device:TPU:1, one launch (start us, length us, event | category | flops | bytes accessed | tf_op | source)
XLA Modules:
  0.0 403.6 jit_solution(9102663855449639479)
XLA Ops:
  10.5 31.3 %collective-permute-done.1 = f32[2,128,512]{2,1,0:T(8,128)S(1)} collective-permute-done((f32[2,128,512]{2,1,0:T(8,128)S(1)}, f32[2,128,512]{2,1,0:T(8,128)S(1)}, u32[]{:S(2)}, u32[]{:S(2)}) %collective-permute-start.1) | collective-permute-done | bytes 524320 | tf_op jit(solution)/shard_map/ppermute | solution.py:17
  41.8 11.2 %collective-permute-done = f32[2,128,512]{2,1,0:T(8,128)S(1)} collective-permute-done((f32[2,128,512]{2,1,0:T(8,128)S(1)}, f32[2,128,512]{2,1,0:T(8,128)S(1)}, u32[]{:S(2)}, u32[]{:S(2)}) %collective-permute-start) | collective-permute-done | bytes 524320 | tf_op jit(solution)/shard_map/ppermute | solution.py:17
  59.2 8.7 %collective-permute-done.2 = f32[2,128,512]{2,1,0:T(8,128)S(1)} collective-permute-done((f32[2,128,512]{2,1,0:T(8,128)S(1)}, f32[2,128,512]{2,1,0:T(8,128)S(1)}, u32[]{:S(2)}, u32[]{:S(2)}) %collective-permute-start.2) | collective-permute-done | bytes 524320 | tf_op jit(solution)/shard_map/ppermute | solution.py:17
  67.9 11.2 %collective-permute-done.3 = f32[2,128,512]{2,1,0:T(8,128)S(1)} collective-permute-done((f32[2,128,512]{2,1,0:T(8,128)S(1)}, f32[2,128,512]{2,1,0:T(8,128)S(1)}, u32[]{:S(2)}, u32[]{:S(2)}) %collective-permute-start.3) | collective-permute-done | bytes 524320 | tf_op jit(solution)/shard_map/ppermute | solution.py:17
  86.6 7.9 %collective-permute-done.4 = f32[2,128,512]{2,1,0:T(8,128)S(1)} collective-permute-done((f32[2,128,512]{2,1,0:T(8,128)S(1)}, f32[2,128,512]{2,1,0:T(8,128)S(1)}, u32[]{:S(2)}, u32[]{:S(2)}) %collective-permute-start.4) | collective-permute-done | bytes 524320 | tf_op jit(solution)/shard_map/ppermute | solution.py:17
  94.5 11.2 %collective-permute-done.5 = f32[2,128,512]{2,1,0:T(8,128)S(1)} collective-permute-done((f32[2,128,512]{2,1,0:T(8,128)S(1)}, f32[2,128,512]{2,1,0:T(8,128)S(1)}, u32[]{:S(2)}, u32[]{:S(2)}) %collective-permute-start.5) | collective-permute-done | bytes 524320 | tf_op jit(solution)/shard_map/ppermute | solution.py:17
  111.5 7.0 %collective-permute-done.6 = f32[2,128,512]{2,1,0:T(8,128)S(1)} collective-permute-done((f32[2,128,512]{2,1,0:T(8,128)S(1)}, f32[2,128,512]{2,1,0:T(8,128)S(1)}, u32[]{:S(2)}, u32[]{:S(2)}) %collective-permute-start.6) | collective-permute-done | bytes 524320 | tf_op jit(solution)/shard_map/ppermute | solution.py:17
  118.5 11.2 %collective-permute-done.7 = f32[2,128,512]{2,1,0:T(8,128)S(1)} collective-permute-done((f32[2,128,512]{2,1,0:T(8,128)S(1)}, f32[2,128,512]{2,1,0:T(8,128)S(1)}, u32[]{:S(2)}, u32[]{:S(2)}) %collective-permute-start.7) | collective-permute-done | bytes 524320 | tf_op jit(solution)/shard_map/ppermute | solution.py:17
  143.1 11.2 %collective-permute-done.9 = f32[2,128,512]{2,1,0:T(8,128)S(1)} collective-permute-done((f32[2,128,512]{2,1,0:T(8,128)S(1)}, f32[2,128,512]{2,1,0:T(8,128)S(1)}, u32[]{:S(2)}, u32[]{:S(2)}) %collective-permute-start.9) | collective-permute-done | bytes 524320 | tf_op jit(solution)/shard_map/ppermute | solution.py:17
  165.2 11.2 %collective-permute-done.11 = f32[2,128,512]{2,1,0:T(8,128)S(1)} collective-permute-done((f32[2,128,512]{2,1,0:T(8,128)S(1)}, f32[2,128,512]{2,1,0:T(8,128)S(1)}, u32[]{:S(2)}, u32[]{:S(2)}) %collective-permute-start.11) | collective-permute-done | bytes 524320 | tf_op jit(solution)/shard_map/ppermute | solution.py:17
  176.8 7.5 %collective-permute-start.12 = (f32[2,128,512]{2,1,0:T(8,128)S(1)}, f32[2,128,512]{2,1,0:T(8,128)S(1)}, u32[]{:S(2)}, u32[]{:S(2)}) collective-permute-start(f32[2,128,512]{2,1,0:T(8,128)S(1)} %get-tuple-element.25), channel_id=1, source_target_pairs={{0,4},{4,0},{8,12},{12,8},{16,20},{20,16},{24,28},{28,24},{32,36},... | collective-permute-start | bytes 1572872 | tf_op jit(solution)/shard_map/ppermute | solution.py:17
  210.1 9.6 %collective-permute-done.16 = f32[2,128,512]{2,1,0:T(8,128)S(1)} collective-permute-done((f32[2,128,512]{2,1,0:T(8,128)S(1)}, f32[2,128,512]{2,1,0:T(8,128)S(1)}, u32[]{:S(2)}, u32[]{:S(2)}) %collective-permute-start.16) | collective-permute-done | bytes 524320 | tf_op jit(solution)/shard_map/ppermute | solution.py:17
  219.7 11.2 %collective-permute-done.17 = f32[2,128,512]{2,1,0:T(8,128)S(1)} collective-permute-done((f32[2,128,512]{2,1,0:T(8,128)S(1)}, f32[2,128,512]{2,1,0:T(8,128)S(1)}, u32[]{:S(2)}, u32[]{:S(2)}) %collective-permute-start.17) | collective-permute-done | bytes 524320 | tf_op jit(solution)/shard_map/ppermute | solution.py:17
  238.2 8.7 %collective-permute-done.18 = f32[2,128,512]{2,1,0:T(8,128)S(1)} collective-permute-done((f32[2,128,512]{2,1,0:T(8,128)S(1)}, f32[2,128,512]{2,1,0:T(8,128)S(1)}, u32[]{:S(2)}, u32[]{:S(2)}) %collective-permute-start.18) | collective-permute-done | bytes 524320 | tf_op jit(solution)/shard_map/ppermute | solution.py:17
  246.8 11.2 %collective-permute-done.19 = f32[2,128,512]{2,1,0:T(8,128)S(1)} collective-permute-done((f32[2,128,512]{2,1,0:T(8,128)S(1)}, f32[2,128,512]{2,1,0:T(8,128)S(1)}, u32[]{:S(2)}, u32[]{:S(2)}) %collective-permute-start.19) | collective-permute-done | bytes 524320 | tf_op jit(solution)/shard_map/ppermute | solution.py:17
  263.8 7.7 %collective-permute-done.20 = f32[2,128,512]{2,1,0:T(8,128)S(1)} collective-permute-done((f32[2,128,512]{2,1,0:T(8,128)S(1)}, f32[2,128,512]{2,1,0:T(8,128)S(1)}, u32[]{:S(2)}, u32[]{:S(2)}) %collective-permute-start.20) | collective-permute-done | bytes 524320 | tf_op jit(solution)/shard_map/ppermute | solution.py:17
  271.5 11.2 %collective-permute-done.21 = f32[2,128,512]{2,1,0:T(8,128)S(1)} collective-permute-done((f32[2,128,512]{2,1,0:T(8,128)S(1)}, f32[2,128,512]{2,1,0:T(8,128)S(1)}, u32[]{:S(2)}, u32[]{:S(2)}) %collective-permute-start.21) | collective-permute-done | bytes 524320 | tf_op jit(solution)/shard_map/ppermute | solution.py:17
  290.2 6.6 %collective-permute-done.22 = f32[2,128,512]{2,1,0:T(8,128)S(1)} collective-permute-done((f32[2,128,512]{2,1,0:T(8,128)S(1)}, f32[2,128,512]{2,1,0:T(8,128)S(1)}, u32[]{:S(2)}, u32[]{:S(2)}) %collective-permute-start.22) | collective-permute-done | bytes 524320 | tf_op jit(solution)/shard_map/ppermute | solution.py:17
  296.8 11.2 %collective-permute-done.23 = f32[2,128,512]{2,1,0:T(8,128)S(1)} collective-permute-done((f32[2,128,512]{2,1,0:T(8,128)S(1)}, f32[2,128,512]{2,1,0:T(8,128)S(1)}, u32[]{:S(2)}, u32[]{:S(2)}) %collective-permute-start.23) | collective-permute-done | bytes 524320 | tf_op jit(solution)/shard_map/ppermute | solution.py:17
  316.1 6.2 %collective-permute-done.24 = f32[2,128,512]{2,1,0:T(8,128)S(1)} collective-permute-done((f32[2,128,512]{2,1,0:T(8,128)S(1)}, f32[2,128,512]{2,1,0:T(8,128)S(1)}, u32[]{:S(2)}, u32[]{:S(2)}) %collective-permute-start.24) | collective-permute-done | bytes 524320 | tf_op jit(solution)/shard_map/ppermute | solution.py:17
  322.3 11.2 %collective-permute-done.25 = f32[2,128,512]{2,1,0:T(8,128)S(1)} collective-permute-done((f32[2,128,512]{2,1,0:T(8,128)S(1)}, f32[2,128,512]{2,1,0:T(8,128)S(1)}, u32[]{:S(2)}, u32[]{:S(2)}) %collective-permute-start.25) | collective-permute-done | bytes 524320 | tf_op jit(solution)/shard_map/ppermute | solution.py:17
  342.7 31.0 %collective-permute-done.26 = f32[2,128,512]{2,1,0:T(8,128)S(1)} collective-permute-done((f32[2,128,512]{2,1,0:T(8,128)S(1)}, f32[2,128,512]{2,1,0:T(8,128)S(1)}, u32[]{:S(2)}, u32[]{:S(2)}) %collective-permute-start.26) | collective-permute-done | bytes 524320 | tf_op jit(solution)/shard_map/ppermute | solution.py:17
  373.7 11.2 %collective-permute-done.27 = f32[2,128,512]{2,1,0:T(8,128)S(1)} collective-permute-done((f32[2,128,512]{2,1,0:T(8,128)S(1)}, f32[2,128,512]{2,1,0:T(8,128)S(1)}, u32[]{:S(2)}, u32[]{:S(2)}) %collective-permute-start.27) | collective-permute-done | bytes 524320 | tf_op jit(solution)/shard_map/ppermute | solution.py:17
  385.9 15.6 %psum.7 = f32[128]{0:T(128)S(1)} all-reduce(f32[128]{0:T(128)S(1)} %get-tuple-element.4), channel_id=1, replica_groups=mesh['context'=128,'tensor'=4] {'tensor'}, use_global_device_ids=true, to_apply=%region_1.2 | all-reduce | flops 128 | bytes 1024 | tf_op jit(solution)/shard_map/psum | solution.py:134
  (91 shorter events, 117.5 us)
Async XLA Ops:
  2.7 39.2 %collective-permute-start.1 = (f32[2,128,512]{2,1,0:T(8,128)S(1)}, f32[2,128,512]{2,1,0:T(8,128)S(1)}, u32[]{:S(2)}, u32[]{:S(2)}) collective-permute-start(f32[2,128,512]{2,1,0:T(8,128)S(1)} %pad_maximum_fusion.1), channel_id=1, source_target_pairs={{0,256},{4,260},{8,264},{12,268},{16,272},{20,276},{24,280},{28,28... | collective-permute-start | bytes 1572872 | tf_op jit(solution)/shard_map/ppermute | solution.py:17
  8.4 44.6 %collective-permute-start = (f32[2,128,512]{2,1,0:T(8,128)S(1)}, f32[2,128,512]{2,1,0:T(8,128)S(1)}, u32[]{:S(2)}, u32[]{:S(2)}) collective-permute-start(f32[2,128,512]{2,1,0:T(8,128)S(1)} %pad_maximum_fusion), channel_id=1, source_target_pairs={{0,256},{4,260},{8,264},{12,268},{16,272},{20,276},{24,280},{28,28... | collective-permute-start | bytes 1572872 | tf_op jit(solution)/shard_map/ppermute | solution.py:17
  53.3 14.6 %collective-permute-start.2 = (f32[2,128,512]{2,1,0:T(8,128)S(1)}, f32[2,128,512]{2,1,0:T(8,128)S(1)}, u32[]{:S(2)}, u32[]{:S(2)}) collective-permute-start(f32[2,128,512]{2,1,0:T(8,128)S(1)} %get-tuple-element.35), channel_id=1, source_target_pairs={{0,128},{4,132},{8,136},{12,140},{16,144},{20,148},{24,152},{28,15... | collective-permute-start | bytes 1572872 | tf_op jit(solution)/shard_map/ppermute | solution.py:17
  57.1 22.0 %collective-permute-start.3 = (f32[2,128,512]{2,1,0:T(8,128)S(1)}, f32[2,128,512]{2,1,0:T(8,128)S(1)}, u32[]{:S(2)}, u32[]{:S(2)}) collective-permute-start(f32[2,128,512]{2,1,0:T(8,128)S(1)} %get-tuple-element.34), channel_id=1, source_target_pairs={{0,128},{4,132},{8,136},{12,140},{16,144},{20,148},{24,152},{28,15... | collective-permute-start | bytes 1572872 | tf_op jit(solution)/shard_map/ppermute | solution.py:17
  79.4 15.1 %collective-permute-start.4 = (f32[2,128,512]{2,1,0:T(8,128)S(1)}, f32[2,128,512]{2,1,0:T(8,128)S(1)}, u32[]{:S(2)}, u32[]{:S(2)}) collective-permute-start(f32[2,128,512]{2,1,0:T(8,128)S(1)} %get-tuple-element.33), channel_id=1, source_target_pairs={{0,64},{4,68},{8,72},{12,76},{16,80},{20,84},{24,88},{28,92},{32,9... | collective-permute-start | bytes 1572872 | tf_op jit(solution)/shard_map/ppermute | solution.py:17
  84.5 21.3 %collective-permute-start.5 = (f32[2,128,512]{2,1,0:T(8,128)S(1)}, f32[2,128,512]{2,1,0:T(8,128)S(1)}, u32[]{:S(2)}, u32[]{:S(2)}) collective-permute-start(f32[2,128,512]{2,1,0:T(8,128)S(1)} %get-tuple-element.32), channel_id=1, source_target_pairs={{0,64},{4,68},{8,72},{12,76},{16,80},{20,84},{24,88},{28,92},{32,9... | collective-permute-start | bytes 1572872 | tf_op jit(solution)/shard_map/ppermute | solution.py:17
  106.0 12.5 %collective-permute-start.6 = (f32[2,128,512]{2,1,0:T(8,128)S(1)}, f32[2,128,512]{2,1,0:T(8,128)S(1)}, u32[]{:S(2)}, u32[]{:S(2)}) collective-permute-start(f32[2,128,512]{2,1,0:T(8,128)S(1)} %get-tuple-element.31), channel_id=1, source_target_pairs={{0,32},{4,36},{8,40},{12,44},{16,48},{20,52},{24,56},{28,60},{32,0... | collective-permute-start | bytes 1572872 | tf_op jit(solution)/shard_map/ppermute | solution.py:17
  109.0 20.7 %collective-permute-start.7 = (f32[2,128,512]{2,1,0:T(8,128)S(1)}, f32[2,128,512]{2,1,0:T(8,128)S(1)}, u32[]{:S(2)}, u32[]{:S(2)}) collective-permute-start(f32[2,128,512]{2,1,0:T(8,128)S(1)} %get-tuple-element.30), channel_id=1, source_target_pairs={{0,32},{4,36},{8,40},{12,44},{16,48},{20,52},{24,56},{28,60},{32,0... | collective-permute-start | bytes 1572872 | tf_op jit(solution)/shard_map/ppermute | solution.py:17
  130.0 13.1 %collective-permute-start.8 = (f32[2,128,512]{2,1,0:T(8,128)S(1)}, f32[2,128,512]{2,1,0:T(8,128)S(1)}, u32[]{:S(2)}, u32[]{:S(2)}) collective-permute-start(f32[2,128,512]{2,1,0:T(8,128)S(1)} %get-tuple-element.29), channel_id=1, source_target_pairs={{0,16},{4,20},{8,24},{12,28},{16,0},{20,4},{24,8},{28,12},{32,48},... | collective-permute-start | bytes 1572872 | tf_op jit(solution)/shard_map/ppermute | solution.py:17
  134.3 20.1 %collective-permute-start.9 = (f32[2,128,512]{2,1,0:T(8,128)S(1)}, f32[2,128,512]{2,1,0:T(8,128)S(1)}, u32[]{:S(2)}, u32[]{:S(2)}) collective-permute-start(f32[2,128,512]{2,1,0:T(8,128)S(1)} %get-tuple-element.28), channel_id=1, source_target_pairs={{0,16},{4,20},{8,24},{12,28},{16,0},{20,4},{24,8},{28,12},{32,48},... | collective-permute-start | bytes 1572872 | tf_op jit(solution)/shard_map/ppermute | solution.py:17
  154.6 10.6 %collective-permute-start.10 = (f32[2,128,512]{2,1,0:T(8,128)S(1)}, f32[2,128,512]{2,1,0:T(8,128)S(1)}, u32[]{:S(2)}, u32[]{:S(2)}) collective-permute-start(f32[2,128,512]{2,1,0:T(8,128)S(1)} %get-tuple-element.27), channel_id=1, source_target_pairs={{0,8},{4,12},{8,0},{12,4},{16,24},{20,28},{24,16},{28,20},{32,40},... | collective-permute-start | bytes 1572872 | tf_op jit(solution)/shard_map/ppermute | solution.py:17
  157.1 19.4 %collective-permute-start.11 = (f32[2,128,512]{2,1,0:T(8,128)S(1)}, f32[2,128,512]{2,1,0:T(8,128)S(1)}, u32[]{:S(2)}, u32[]{:S(2)}) collective-permute-start(f32[2,128,512]{2,1,0:T(8,128)S(1)} %get-tuple-element.26), channel_id=1, source_target_pairs={{0,8},{4,12},{8,0},{12,4},{16,24},{20,28},{24,16},{28,20},{32,40},... | collective-permute-start | bytes 1572872 | tf_op jit(solution)/shard_map/ppermute | solution.py:17
  204.7 15.0 %collective-permute-start.16 = (f32[2,128,512]{2,1,0:T(8,128)S(1)}, f32[2,128,512]{2,1,0:T(8,128)S(1)}, u32[]{:S(2)}, u32[]{:S(2)}) collective-permute-start(f32[2,128,512]{2,1,0:T(8,128)S(1)} %get-tuple-element.18), channel_id=1, source_target_pairs={{0,8},{4,12},{8,0},{12,4},{16,24},{20,28},{24,16},{28,20},{32,40},... | collective-permute-start | bytes 1572872 | tf_op jit(solution)/shard_map/ppermute | solution.py:17
  207.1 23.8 %collective-permute-start.17 = (f32[2,128,512]{2,1,0:T(8,128)S(1)}, f32[2,128,512]{2,1,0:T(8,128)S(1)}, u32[]{:S(2)}, u32[]{:S(2)}) collective-permute-start(f32[2,128,512]{2,1,0:T(8,128)S(1)} %get-tuple-element.19), channel_id=1, source_target_pairs={{0,8},{4,12},{8,0},{12,4},{16,24},{20,28},{24,16},{28,20},{32,40},... | collective-permute-start | bytes 1572872 | tf_op jit(solution)/shard_map/ppermute | solution.py:17
  231.2 15.6 %collective-permute-start.18 = (f32[2,128,512]{2,1,0:T(8,128)S(1)}, f32[2,128,512]{2,1,0:T(8,128)S(1)}, u32[]{:S(2)}, u32[]{:S(2)}) collective-permute-start(f32[2,128,512]{2,1,0:T(8,128)S(1)} %get-tuple-element.16), channel_id=1, source_target_pairs={{0,16},{4,20},{8,24},{12,28},{16,0},{20,4},{24,8},{28,12},{32,48},... | collective-permute-start | bytes 1572872 | tf_op jit(solution)/shard_map/ppermute | solution.py:17
  235.2 22.9 %collective-permute-start.19 = (f32[2,128,512]{2,1,0:T(8,128)S(1)}, f32[2,128,512]{2,1,0:T(8,128)S(1)}, u32[]{:S(2)}, u32[]{:S(2)}) collective-permute-start(f32[2,128,512]{2,1,0:T(8,128)S(1)} %get-tuple-element.17), channel_id=1, source_target_pairs={{0,16},{4,20},{8,24},{12,28},{16,0},{20,4},{24,8},{28,12},{32,48},... | collective-permute-start | bytes 1572872 | tf_op jit(solution)/shard_map/ppermute | solution.py:17
  258.4 13.2 %collective-permute-start.20 = (f32[2,128,512]{2,1,0:T(8,128)S(1)}, f32[2,128,512]{2,1,0:T(8,128)S(1)}, u32[]{:S(2)}, u32[]{:S(2)}) collective-permute-start(f32[2,128,512]{2,1,0:T(8,128)S(1)} %get-tuple-element.14), channel_id=1, source_target_pairs={{0,32},{4,36},{8,40},{12,44},{16,48},{20,52},{24,56},{28,60},{32,0... | collective-permute-start | bytes 1572872 | tf_op jit(solution)/shard_map/ppermute | solution.py:17
  260.9 21.9 %collective-permute-start.21 = (f32[2,128,512]{2,1,0:T(8,128)S(1)}, f32[2,128,512]{2,1,0:T(8,128)S(1)}, u32[]{:S(2)}, u32[]{:S(2)}) collective-permute-start(f32[2,128,512]{2,1,0:T(8,128)S(1)} %get-tuple-element.15), channel_id=1, source_target_pairs={{0,32},{4,36},{8,40},{12,44},{16,48},{20,52},{24,56},{28,60},{32,0... | collective-permute-start | bytes 1572872 | tf_op jit(solution)/shard_map/ppermute | solution.py:17
  283.1 13.8 %collective-permute-start.22 = (f32[2,128,512]{2,1,0:T(8,128)S(1)}, f32[2,128,512]{2,1,0:T(8,128)S(1)}, u32[]{:S(2)}, u32[]{:S(2)}) collective-permute-start(f32[2,128,512]{2,1,0:T(8,128)S(1)} %get-tuple-element.12), channel_id=1, source_target_pairs={{0,64},{4,68},{8,72},{12,76},{16,80},{20,84},{24,88},{28,92},{32,9... | collective-permute-start | bytes 1572872 | tf_op jit(solution)/shard_map/ppermute | solution.py:17
  287.2 20.9 %collective-permute-start.23 = (f32[2,128,512]{2,1,0:T(8,128)S(1)}, f32[2,128,512]{2,1,0:T(8,128)S(1)}, u32[]{:S(2)}, u32[]{:S(2)}) collective-permute-start(f32[2,128,512]{2,1,0:T(8,128)S(1)} %get-tuple-element.13), channel_id=1, source_target_pairs={{0,64},{4,68},{8,72},{12,76},{16,80},{20,84},{24,88},{28,92},{32,9... | collective-permute-start | bytes 1572872 | tf_op jit(solution)/shard_map/ppermute | solution.py:17
  308.3 13.9 %collective-permute-start.24 = (f32[2,128,512]{2,1,0:T(8,128)S(1)}, f32[2,128,512]{2,1,0:T(8,128)S(1)}, u32[]{:S(2)}, u32[]{:S(2)}) collective-permute-start(f32[2,128,512]{2,1,0:T(8,128)S(1)} %get-tuple-element.10), channel_id=1, source_target_pairs={{0,128},{4,132},{8,136},{12,140},{16,144},{20,148},{24,152},{28,15... | collective-permute-start | bytes 1572872 | tf_op jit(solution)/shard_map/ppermute | solution.py:17
  314.0 19.5 %collective-permute-start.25 = (f32[2,128,512]{2,1,0:T(8,128)S(1)}, f32[2,128,512]{2,1,0:T(8,128)S(1)}, u32[]{:S(2)}, u32[]{:S(2)}) collective-permute-start(f32[2,128,512]{2,1,0:T(8,128)S(1)} %get-tuple-element.11), channel_id=1, source_target_pairs={{0,128},{4,132},{8,136},{12,140},{16,144},{20,148},{24,152},{28,15... | collective-permute-start | bytes 1572872 | tf_op jit(solution)/shard_map/ppermute | solution.py:17
  333.8 40.0 %collective-permute-start.26 = (f32[2,128,512]{2,1,0:T(8,128)S(1)}, f32[2,128,512]{2,1,0:T(8,128)S(1)}, u32[]{:S(2)}, u32[]{:S(2)}) collective-permute-start(f32[2,128,512]{2,1,0:T(8,128)S(1)} %get-tuple-element.8), channel_id=1, source_target_pairs={{0,256},{4,260},{8,264},{12,268},{16,272},{20,276},{24,280},{28,28... | collective-permute-start | bytes 1572872 | tf_op jit(solution)/shard_map/ppermute | solution.py:17
  339.8 45.2 %collective-permute-start.27 = (f32[2,128,512]{2,1,0:T(8,128)S(1)}, f32[2,128,512]{2,1,0:T(8,128)S(1)}, u32[]{:S(2)}, u32[]{:S(2)}) collective-permute-start(f32[2,128,512]{2,1,0:T(8,128)S(1)} %get-tuple-element.9), channel_id=1, source_target_pairs={{0,256},{4,260},{8,264},{12,268},{16,272},{20,276},{24,280},{28,28... | collective-permute-start | bytes 1572872 | tf_op jit(solution)/shard_map/ppermute | solution.py:17
  (8 other events, 74.3 us)
where the time goes:
time: 406 us; the launch traced here: 404 us
  waiting for transfers between devices  273 us (67%)
  starting transfers between devices  91.4 us (23%)
  blocking collectives  15.6 us (4%)
  matrix products  8.92 us (2%)
  other arithmetic  5.79 us (1%)
  local copies, waits for them, and re-layouts  4.92 us (1%)
    ppermute x28, waiting for transfers between devices, swapped(): lax.ppermute(value, axis, [(i, i ^ 1 << distance) for i in range(lax.axis...  273 us
    ppermute x28, starting transfers between devices, swapped(): lax.ppermute(value, axis, [(i, i ^ 1 << distance) for i in range(lax.axis...  91.4 us
    psum x1, blocking collectives, on_device(): squares = lax.psum(jnp.sum(gated_mix * gated_mix, axis=1), 'tensor')  15.6 us
    dot_general x8, matrix products, einsum_high(): jnp.einsum(formula, left, right, precision=HIGHEST, preferred_element_typ...  8.92 us
  transfers between devices with their start and end apart: 28, of which 26 were waited for; matrix products, arithmetic and copies ran while one was open for 0% of the time, Pallas kernels for 0%

commit v1 on v0

v1 whole, which is shorter than its diff:
```python
import functools

import jax
import jax.numpy as jnp
import ml_dtypes
import numpy as np
from jax import lax
from jax.experimental import pallas as pl
from jax.experimental.pallas import tpu as pltpu
from jax.sharding import PartitionSpec as P

MESH = pl.DeviceIdType.MESH
F32, BF16 = jnp.float32, jnp.bfloat16

CHANNELS = 4096
TOK = 128
CTX = 128
TEN = 4
FREQS = 2 * TOK * CTX
LOCAL = CHANNELS // TEN
OWN = LOCAL // CTX
PARTS = 1
PC = OWN // PARTS
HALF = CTX // 2
LOW = 8
HIGH = CTX // LOW
EPSILON = 1e-06


def two_terms(table):
    high = table.astype(ml_dtypes.bfloat16)
    low = (table - high.astype(np.float64)).astype(ml_dtypes.bfloat16)
    return high, low


def tables():
    f = np.concatenate([np.arange(0, CTX, 2), np.arange(1, CTX, 2)]).astype(np.float64)
    a = np.arange(CTX, dtype=np.float64)
    first = 2 * np.pi * f[:, None] * a[None, :] / (2 * CTX)
    forward_a = np.concatenate([np.cos(first), -np.sin(first)], axis=0)
    a_high, a_low = two_terms(forward_a)
    a_high = np.concatenate([a_high, a_high], axis=1)
    twist = 2 * np.pi * f[:, None] * a[None, :] / FREQS
    weight = np.where(f == 0, 1.0, 2.0)[:, None] / FREQS
    edge = 2 * np.pi * CTX * a / FREQS
    turn = np.stack([np.cos(twist), np.sin(twist), np.cos(twist) * weight, np.sin(twist) * weight])
    edges = np.stack([np.cos(edge), np.sin(edge), np.cos(edge) / FREQS, np.sin(edge) / FREQS])
    edges = np.repeat(edges[:, None, :], 16, axis=1)
    second = 2 * np.pi * a[:, None] * a[None, :] / TOK
    cos, sin = np.cos(second), np.sin(second)
    forward_j = two_terms(np.block([[cos, -sin], [sin, cos]]))
    inverse_j = two_terms(np.block([[cos, sin], [-sin, cos]]))
    inverse_a = two_terms(np.concatenate([np.cos(first.T), -np.sin(first.T)], axis=1))
    sign = np.repeat(np.where(a % 2 == 0, 1.0, -1.0)[:, None], TOK, axis=1)
    return (
        a_high,
        a_low,
        turn.astype(np.float32),
        edges.astype(np.float32),
        np.stack(forward_j),
        np.stack(inverse_j),
        np.concatenate(inverse_a, axis=0),
        sign.astype(np.float32),
    )


def split(value):
    high = value.astype(BF16)
    return high, (value - high.astype(F32)).astype(BF16)


def dot(left, right):
    return jnp.dot(left, right, preferred_element_type=F32)


def three_products(value, pair):
    rows = value.shape[0]
    high, low = split(value)
    both = dot(jnp.concatenate([high, low], axis=0), pair[0])
    return both[:rows] + both[rows:] + dot(high, pair[1])


def reversed_index(position):
    flipped = 0
    for place in range(7):
        flipped = flipped + ((position >> place) & 1) * (1 << (6 - place))
    return flipped


def mixer(
    query, key, value, spectrum, a_fwd, a_low, turn, edges, j_fwd, j_inv, a_inv, sign,
    gated, scale,
    sending, arrived, answer, result, query_t, pieces, response, squares,
    send_sem, recv_sem, back_send, back_recv, filt_send, filt_recv, sq_send, sq_recv, own_sem, ready,
):
    me = lax.axis_index("context")
    mine = lax.axis_index("tensor")
    my_high, my_low = me // LOW, me % LOW

    def device(high, low):
        return (my_high ^ high) * LOW + (my_low ^ low)

    barrier = pltpu.get_barrier_semaphore()
    for low in range(1, LOW):
        pl.semaphore_signal(barrier, inc=1, device_id=(device(0, low), mine), device_id_type=MESH)
    for high in range(1, HIGH):
        pl.semaphore_signal(barrier, inc=1, device_id=(device(high, 0), mine), device_id_type=MESH)
    for step in range(1, TEN):
        pl.semaphore_signal(barrier, inc=1, device_id=(me, mine ^ step), device_id_type=MESH)

    for block in range(LOCAL // 128):
        columns = pl.ds(block * 128, 128)
        driven = key[:, columns].astype(F32) * value[:, columns].astype(F32)
        sending[columns, :] = driven.T

    pl.semaphore_wait(barrier, LOW - 1 + HIGH - 1 + TEN - 1)
    for low in range(1, LOW):
        pl.semaphore_signal(ready.at[low], inc=1, device_id=(device(0, low), mine), device_id_type=MESH)

    def rows_of(start, count):
        return pl.ds(pl.multiple_of(start * count, count), count)

    def exchange(part, low, first):
        def step(high, carry):
            target = device(high, low)
            pltpu.make_async_remote_copy(
                src_ref=sending.at[rows_of(target * PARTS + part, PC)],
                dst_ref=arrived.at[part, rows_of(me, PC)],
                send_sem=send_sem.at[part],
                recv_sem=recv_sem.at[part],
                device_id=(target, mine),
                device_id_type=MESH,
            ).start()
            return carry

        lax.fori_loop(first, HIGH, step, 0)

    own = [
        pltpu.make_async_copy(
            sending.at[rows_of(me * PARTS + part, PC)], arrived.at[part, rows_of(me, PC)], own_sem.at[part]
        )
        for part in range(PARTS)
    ]
    for part in range(PARTS):
        own[part].start()
        for low in range(LOW):
            if low and not part:
                pl.semaphore_wait(ready.at[low], 1)
            exchange(part, low, 0 if low else 1)

    order = reversed_index(me)
    holds = order <= HALF
    for kind in range(4):
        pieces[pl.ds(kind, LOCAL // 16, stride=4), :] = spectrum[kind // 2, kind % 2]

    def filter_copy(target):
        return pltpu.make_async_remote_copy(
            src_ref=pieces.at[rows_of(target // 2, 4)],
            dst_ref=response.at[rows_of(order, 4)],
            send_sem=filt_send,
            recv_sem=filt_recv,
            device_id=(target, mine),
            device_id_type=MESH,
        )

    @pl.when(holds)
    def _():
        def step(other, carry):
            filter_copy(me ^ other).start()
            return carry

        lax.fori_loop(1, CTX, step, 0)
        local = pltpu.make_async_copy(
            pieces.at[rows_of(me // 2, 4)], response.at[rows_of(order, 4)], own_sem.at[PARTS]
        )
        local.start()
        local.wait()

    for block in range(LOCAL // 128):
        columns = pl.ds(block * 128, 128)
        query_t[columns, :] = query[:, columns].astype(F32).T

    def wait_rows(ref, count, sem):
        pltpu.make_async_copy(ref.at[pl.ds(0, count)], ref.at[pl.ds(0, count)], sem).wait()

    for part in range(PARTS):
        own[part].wait()
        wait_rows(arrived.at[part], (CTX - 1) * PC, recv_sem.at[part])

        block = arrived[part].reshape(CTX // 2, 2 * PC, TOK)
        folded = jnp.sum(block, axis=0)
        edge = folded[:PC] - folded[PC:]
        edge = jnp.concatenate([edge, jnp.zeros((16 - PC, TOK), F32)], axis=0)
        edge = jnp.concatenate([edge * edges[0], -edge * edges[1]], axis=1)
        edge = three_products(edge, j_fwd)

        if part == 0:

            @pl.when(holds)
            def _():
                wait_rows(response, HALF * 4, filt_recv)

            @pl.when(jnp.logical_not(holds))
            def _():
                wait_rows(response, (HALF + 1) * 4, filt_recv)

        h_re = jnp.concatenate([response[pl.ds(kind, HALF, stride=4), :] for kind in (0, 1)], axis=0)
        h_im = jnp.concatenate([response[pl.ds(kind, HALF, stride=4), :] for kind in (2, 3)], axis=0)
        e_re, e_im = response[pl.ds(4 * HALF, 1), :], response[pl.ds(4 * HALF + 2, 1), :]
        z_re, z_im = edge[:, :TOK], edge[:, TOK:]
        edge = jnp.concatenate([z_re * e_re - z_im * e_im, z_re * e_im + z_im * e_re], axis=1)
        edge = three_products(edge, j_inv)
        edge = edge[:, :TOK] * edges[2] - edge[:, TOK:] * edges[3]

        for pair in range(PC // 2):
            high, low = split(
                jnp.concatenate(
                    [arrived[part, pl.ds(2 * pair + k, CTX, stride=PC), :] for k in (0, 1)], axis=1
                )
            )
            freq = dot(a_fwd[...], jnp.concatenate([high, low], axis=0)) + dot(a_low[...], high)
            rows = []
            for k in (0, 1):
                y_re, y_im = freq[:CTX, k * TOK : (k + 1) * TOK], freq[CTX:, k * TOK : (k + 1) * TOK]
                rows.append(
                    jnp.concatenate([y_re * turn[0] + y_im * turn[1], y_im * turn[0] - y_re * turn[1]], axis=1)
                )
            freq = three_products(jnp.concatenate(rows, axis=0), j_fwd)
            rows = []
            for k in (0, 1):
                z_re, z_im = freq[k * CTX : (k + 1) * CTX, :TOK], freq[k * CTX : (k + 1) * CTX, TOK:]
                rows.append(jnp.concatenate([z_re * h_re - z_im * h_im, z_re * h_im + z_im * h_re], axis=1))
            back = three_products(jnp.concatenate(rows, axis=0), j_inv)
            columns = []
            for k in (0, 1):
                u_re, u_im = back[k * CTX : (k + 1) * CTX, :TOK], back[k * CTX : (k + 1) * CTX, TOK:]
                columns.append(
                    jnp.concatenate([u_re * turn[2] - u_im * turn[3], u_im * turn[2] + u_re * turn[3]], axis=0)
                )
            high, low = split(jnp.concatenate(columns, axis=1))
            both = dot(a_inv[...], high)
            back = both[:CTX] + both[CTX:] + dot(a_inv[:CTX], low)
            for k in (0, 1):
                channel = 2 * pair + k
                answer[part, pl.ds(channel, CTX, stride=PC), :] = (
                    back[:, k * TOK : (k + 1) * TOK] + sign[...] * edge[channel : channel + 1]
                )

        def step(other, carry):
            target = me ^ other
            pltpu.make_async_remote_copy(
                src_ref=answer.at[part, rows_of(target, PC)],
                dst_ref=result.at[rows_of(me * PARTS + part, PC)],
                send_sem=back_send,
                recv_sem=back_recv,
                device_id=(target, mine),
                device_id_type=MESH,
            ).start()
            return carry

        lax.fori_loop(1, CTX, step, 0)
        local = pltpu.make_async_copy(
            answer.at[part, rows_of(me, PC)], result.at[rows_of(me * PARTS + part, PC)], own_sem.at[part]
        )
        local.start()
        local.wait()

    wait_rows(result, (CTX - 1) * OWN, back_recv)
    total = jnp.zeros((8, TOK), F32)
    for block in range(LOCAL // 128):
        rows = pl.ds(block * 128, 128)
        mix = query_t[rows, :] * result[rows, :]
        gated[rows, :] = mix
        total = total + jnp.sum((mix * mix).reshape(16, 8, TOK), axis=0)
    squares[mine] = jnp.broadcast_to(jnp.sum(total, axis=0, keepdims=True), (8, TOK))
    copies = [
        pltpu.make_async_remote_copy(
            src_ref=squares.at[mine],
            dst_ref=squares.at[mine],
            send_sem=sq_send.at[step],
            recv_sem=sq_recv.at[step],
            device_id=(me, mine ^ step),
            device_id_type=MESH,
        )
        for step in range(1, TEN)
    ]
    for copy in copies:
        copy.start()
    for part in range(PARTS):
        wait_rows(sending, (CTX - 1) * PC, send_sem.at[part])
    wait_rows(sending, (CTX - 1) * OWN, back_send)

    @pl.when(holds)
    def _():
        wait_rows(sending, (CTX - 1) * 4, filt_send)

    for copy in copies:
        copy.wait()
    mean = (squares[0] + squares[1] + squares[2] + squares[3]) / CHANNELS
    scale[...] = lax.rsqrt(mean + EPSILON)


def finish(mixed, scale, gain, gated, normed):
    column = scale[...].T[:, 0:1]
    value = mixed[...].T
    gated[...] = value
    normed[...] = (value * column * gain[...].astype(F32)).astype(BF16)


def on_device(query_gate, key_branch, value_branch, filter_spectrum, norm_gain):
    vmem = pl.BlockSpec(memory_space=pltpu.VMEM)
    constants = [jnp.asarray(table) for table in tables()]
    mixed, scale = pl.pallas_call(
        mixer,
        out_shape=(
            jax.ShapeDtypeStruct((LOCAL, TOK), F32),
            jax.ShapeDtypeStruct((8, TOK), F32),
        ),
        in_specs=[vmem] * (4 + len(constants)),
        out_specs=(vmem, vmem),
        scratch_shapes=[
            pltpu.VMEM((LOCAL, TOK), F32),
            pltpu.VMEM((PARTS, CTX * PC, TOK), F32),
            pltpu.VMEM((PARTS, CTX * PC, TOK), F32),
            pltpu.VMEM((LOCAL, TOK), F32),
            pltpu.VMEM((LOCAL, TOK), F32),
            pltpu.VMEM((LOCAL // 16 * 4, TOK), F32),
            pltpu.VMEM(((HALF + 2) * 4, TOK), F32),
            pltpu.VMEM((TEN, 8, TOK), F32),
            pltpu.SemaphoreType.DMA((PARTS,)),
            pltpu.SemaphoreType.DMA((PARTS,)),
            pltpu.SemaphoreType.DMA,
            pltpu.SemaphoreType.DMA,
            pltpu.SemaphoreType.DMA,
            pltpu.SemaphoreType.DMA,
            pltpu.SemaphoreType.DMA((TEN,)),
            pltpu.SemaphoreType.DMA((TEN,)),
            pltpu.SemaphoreType.DMA((PARTS + 1,)),
            pltpu.SemaphoreType.REGULAR((LOW,)),
        ],
        compiler_params=pltpu.CompilerParams(
            collective_id=0, has_side_effects=True, vmem_limit_bytes=48 << 20
        ),
    )(query_gate, key_branch, value_branch, filter_spectrum.reshape(2, 2, -1, TOK), *constants)
    blocks = 4
    wide = LOCAL // blocks
    return pl.pallas_call(
        finish,
        grid=(blocks,),
        out_shape=(
            jax.ShapeDtypeStruct((TOK, LOCAL), F32),
            jax.ShapeDtypeStruct((TOK, LOCAL), BF16),
        ),
        in_specs=[
            pl.BlockSpec((wide, TOK), lambda i: (i, 0)),
            pl.BlockSpec((8, TOK), lambda i: (0, 0)),
            pl.BlockSpec((1, wide), lambda i: (0, i)),
        ],
        out_specs=(
            pl.BlockSpec((TOK, wide), lambda i: (0, i)),
            pl.BlockSpec((TOK, wide), lambda i: (0, i)),
        ),
        compiler_params=pltpu.CompilerParams(vmem_limit_bytes=16 << 20),
    )(mixed, scale, norm_gain.reshape(1, LOCAL))


def solution(mesh):
    placed = (
        P("context", "tensor"),
        P("context", "tensor"),
        P("context", "tensor"),
        P("context", None, None, "tensor", None),
        P("tensor"),
    )
    return jax.shard_map(
        on_device,
        mesh=mesh,
        in_specs=placed,
        out_specs=(P("context", "tensor"), P("context", "tensor")),
        check_vma=False,
    )
```

time: 406 us -> 73.9 us (0.18)
  waiting for transfers between devices: 273 us -> 0 us
  starting transfers between devices: 91.4 us -> 0 us
  Pallas kernels: 0 us -> 60.3 us
  blocking collectives: 15.6 us -> 0 us
  matrix products: 8.92 us -> 0 us
  local copies, waits for them, and re-layouts: 4.92 us -> 11.5 us
  other arithmetic: 5.79 us -> 0 us
    ppermute x28 -> x0, waiting for transfers between devices: 273 us -> none  [swapped(): lax.ppermute(value, axis, [(i, i ^ 1 << distance) for i in range(lax.axis...]
    ppermute x28 -> x0, starting transfers between devices: 91.4 us -> none  [swapped(): lax.ppermute(value, axis, [(i, i ^ 1 << distance) for i in range(lax.axis...]
    pallas_call x0 -> x2, Pallas kernels: none -> 60.3 us  [the longest x1 58.5 us: on_device(): pl.pallas_call(mixer, out_shape=(jax.ShapeDtypeStruct((LOCAL, TOK), F32),...]
    psum x1 -> x0, blocking collectives: 15.6 us -> none  [on_device(): squares = lax.psum(jnp.sum(gated_mix * gated_mix, axis=1), 'tensor')]
    dot_general x8 -> x0, matrix products: 8.92 us -> none  [einsum_high(): jnp.einsum(formula, left, right, precision=HIGHEST, preferred_element_typ...]
    unnamed x13 -> x24, local copies, waits for them, and re-layouts: 3.86 us -> 10.8 us
    select_n x14 -> x0, other arithmetic: 4.99 us -> none  [the longest x7 3.05 us: on_device(): work_im = jnp.where(upper_half, diff_im, low_im + high_im)]
  transfers between devices with their start and end apart: 28 -> 0, of which waited for: 26 -> 0; matrix products, arithmetic and copies ran while one was open for 0% -> 0% of each run, Pallas kernels for 0% -> 0%
where the time goes in v1:
time: 73.9 us; the launch traced here: 72.5 us
  Pallas kernels  60.3 us (82%)
  local copies, waits for them, and re-layouts  11.5 us (16%)
    pallas_call x1, Pallas kernels, on_device(): pl.pallas_call(mixer, out_shape=(jax.ShapeDtypeStruct((LOCAL, TOK), F32),...  58.5 us
    unnamed x24, local copies, waits for them, and re-layouts  10.8 us
    pallas_call x1, Pallas kernels, on_device(): pl.pallas_call(finish, grid=(blocks,), out_shape=(jax.ShapeDtypeStruct((T...  1.82 us

profile of v1, /device:TPU:1, one launch (start us, length us, event | category | flops | bytes accessed | tf_op | source)
XLA Modules:
  0.0 72.5 jit_solution(17972793408075326029)
XLA Ops:
  0.6 0.7 reshape.11.gain
  1.3 0.0 copy-start
  1.3 0.9 %copy-done = bf16[128,1024]{1,0:T(8,128)(2,1)S(1)} copy-done((bf16[128,1024]{1,0:T(8,128)(2,1)S(1)}, bf16[128,1024]{1,0:T(8,128)(2,1)}, u32[]{:S(2)}) %copy-start) | copy-done | bytes 262168
  2.3 0.0 copy-start.1
  2.3 0.9 %copy-done.1 = bf16[128,1024]{1,0:T(8,128)(2,1)S(1)} copy-done((bf16[128,1024]{1,0:T(8,128)(2,1)S(1)}, bf16[128,1024]{1,0:T(8,128)(2,1)}, u32[]{:S(2)}) %copy-start.1) | copy-done | bytes 262168
  3.2 0.0 copy-start.2
  3.2 0.9 %copy-done.2 = bf16[128,1024]{1,0:T(8,128)(2,1)S(1)} copy-done((bf16[128,1024]{1,0:T(8,128)(2,1)S(1)}, bf16[128,1024]{1,0:T(8,128)(2,1)}, u32[]{:S(2)}) %copy-start.2) | copy-done | bytes 262168
  4.2 0.0 copy-start.3
  4.2 0.9 %copy-done.3 = bf16[2,256,256]{2,1,0:T(8,128)(2,1)S(1)} copy-done((bf16[2,256,256]{2,1,0:T(8,128)(2,1)S(1)}, bf16[2,256,256]{2,1,0:T(8,128)(2,1)}, u32[]{:S(2)}) %copy-start.3) | copy-done | bytes 262168
  5.1 0.0 copy-start.4
  5.1 0.9 %copy-done.4 = bf16[2,256,256]{2,1,0:T(8,128)(2,1)S(1)} copy-done((bf16[2,256,256]{2,1,0:T(8,128)(2,1)S(1)}, bf16[2,256,256]{2,1,0:T(8,128)(2,1)}, u32[]{:S(2)}) %copy-start.4) | copy-done | bytes 262168
  6.1 0.0 copy-start.5
  6.1 0.9 %copy-done.5 = f32[4,128,128]{2,1,0:T(8,128)S(1)} copy-done((f32[4,128,128]{2,1,0:T(8,128)S(1)}, f32[4,128,128]{2,1,0:T(8,128)}, u32[]{:S(2)}) %copy-start.5) | copy-done | bytes 262168
  7.0 0.0 copy-start.6
  7.0 0.9 %copy-done.6 = f32[1,2,2,64,128]{4,3,2,1,0:T(8,128)S(1)} copy-done((f32[1,2,2,64,128]{4,3,2,1,0:T(8,128)S(1)}, f32[1,2,2,64,128]{4,3,2,1,0:T(8,128)}, u32[]{:S(2)}) %copy-start.6) | copy-done | bytes 131096
  7.9 0.0 copy-start.7
  7.9 0.9 %copy-done.7 = bf16[256,256]{1,0:T(8,128)(2,1)S(1)} copy-done((bf16[256,256]{1,0:T(8,128)(2,1)S(1)}, bf16[256,256]{1,0:T(8,128)(2,1)}, u32[]{:S(2)}) %copy-start.7) | copy-done | bytes 131096
  8.8 0.0 copy-start.8
  8.8 0.9 %copy-done.8 = bf16[256,256]{1,0:T(8,128)(2,1)S(1)} copy-done((bf16[256,256]{1,0:T(8,128)(2,1)S(1)}, bf16[256,256]{1,0:T(8,128)(2,1)}, u32[]{:S(2)}) %copy-start.8) | copy-done | bytes 131096
  9.7 0.8 %copy-done.9 = f32[128,128]{1,0:T(8,128)S(1)} copy-done((f32[128,128]{1,0:T(8,128)S(1)}, f32[128,128]{1,0:T(8,128)}, u32[]{:S(2)}) %copy-start.9) | copy-done | bytes 65560
  10.6 0.8 %copy-done.10 = bf16[256,128]{1,0:T(8,128)(2,1)S(1)} copy-done((bf16[256,128]{1,0:T(8,128)(2,1)S(1)}, bf16[256,128]{1,0:T(8,128)(2,1)}, u32[]{:S(2)}) %copy-start.10) | copy-done | bytes 65560
  11.4 0.8 %copy-done.11 = f32[4,16,128]{2,1,0:T(8,128)S(1)} copy-done((f32[4,16,128]{2,1,0:T(8,128)S(1)}, f32[4,16,128]{2,1,0:T(8,128)}, u32[]{:S(2)}) %copy-start.11) | copy-done | bytes 32792
  12.2 58.5 %shard_map.140 = (f32[1024,128]{1,0:T(8,128)S(1)}, f32[8,128]{1,0:T(8,128)S(1)}) custom-call(bf16[128,1024]{1,0:T(8,128)(2,1)S(1)} %copy-done, bf16[128,1024]{1,0:T(8,128)(2,1)S(1)} %copy-done.1, bf16[128,1024]{1,0:T(8,128)(2,1)S(1)} %copy-done.2, f32[2,2,64,128]{3,2,1,0:T(8,128)S(1)} %bitcast.1, bf16[256,256]{1,0:T(8,128)(2,1)S(1)} %copy-done.8, ...), custom_call_target="tpu_custom_call" | custom-call | tf_op jit(solution)/shard_map/pallas_call | solution.py:313
  70.7 1.8 %shard_map.141 = (f32[128,1024]{1,0:T(8,128)}, bf16[128,1024]{1,0:T(8,128)(2,1)}) custom-call(f32[1024,128]{1,0:T(8,128)S(1)} %get-tuple-element.4.mixed, f32[8,128]{1,0:T(8,128)S(1)} %get-tuple-element.5.scale, bf16[1,1024]{1,0:T(2,128)(2,1)S(1)} %reshape.11.gain), custom_call_target="tpu_custom_call" | custom-call | tf_op jit(solution)/shard_map/pallas_call | solution.py:347
  (3 shorter events, 0.0 us)
Async XLA Ops:
  1.3 0.9 %copy-start = (bf16[128,1024]{1,0:T(8,128)(2,1)S(1)}, bf16[128,1024]{1,0:T(8,128)(2,1)}, u32[]{:S(2)}) copy-start(bf16[128,1024]{1,0:T(8,128)(2,1)} %query.1) | copy-start | bytes 786436
  2.3 0.9 %copy-start.1 = (bf16[128,1024]{1,0:T(8,128)(2,1)S(1)}, bf16[128,1024]{1,0:T(8,128)(2,1)}, u32[]{:S(2)}) copy-start(bf16[128,1024]{1,0:T(8,128)(2,1)} %key.1) | copy-start | bytes 786436
  3.2 0.9 %copy-start.2 = (bf16[128,1024]{1,0:T(8,128)(2,1)S(1)}, bf16[128,1024]{1,0:T(8,128)(2,1)}, u32[]{:S(2)}) copy-start(bf16[128,1024]{1,0:T(8,128)(2,1)} %value.1) | copy-start | bytes 786436
  4.2 0.9 %copy-start.3 = (bf16[2,256,256]{2,1,0:T(8,128)(2,1)S(1)}, bf16[2,256,256]{2,1,0:T(8,128)(2,1)}, u32[]{:S(2)}) copy-start(bf16[2,256,256]{2,1,0:T(8,128)(2,1)} %constant.21.clone.j_inv) | copy-start | bytes 786436
  5.1 0.9 %copy-start.4 = (bf16[2,256,256]{2,1,0:T(8,128)(2,1)S(1)}, bf16[2,256,256]{2,1,0:T(8,128)(2,1)}, u32[]{:S(2)}) copy-start(bf16[2,256,256]{2,1,0:T(8,128)(2,1)} %constant.20.clone.j_fwd) | copy-start | bytes 786436
  6.1 0.9 %copy-start.5 = (f32[4,128,128]{2,1,0:T(8,128)S(1)}, f32[4,128,128]{2,1,0:T(8,128)}, u32[]{:S(2)}) copy-start(f32[4,128,128]{2,1,0:T(8,128)} %constant.18.clone.turn) | copy-start | bytes 786436
  7.0 0.9 %copy-start.6 = (f32[1,2,2,64,128]{4,3,2,1,0:T(8,128)S(1)}, f32[1,2,2,64,128]{4,3,2,1,0:T(8,128)}, u32[]{:S(2)}) copy-start(f32[1,2,2,64,128]{4,3,2,1,0:T(8,128)} %param.16) | copy-start | bytes 393220
  7.9 0.9 %copy-start.7 = (bf16[256,256]{1,0:T(8,128)(2,1)S(1)}, bf16[256,256]{1,0:T(8,128)(2,1)}, u32[]{:S(2)}) copy-start(bf16[256,256]{1,0:T(8,128)(2,1)} %constant.22.clone.a_inv) | copy-start | bytes 393220
  8.8 0.9 %copy-start.8 = (bf16[256,256]{1,0:T(8,128)(2,1)S(1)}, bf16[256,256]{1,0:T(8,128)(2,1)}, u32[]{:S(2)}) copy-start(bf16[256,256]{1,0:T(8,128)(2,1)} %constant.16.clone.a_fwd) | copy-start | bytes 393220
  9.7 0.8 %copy-start.9 = (f32[128,128]{1,0:T(8,128)S(1)}, f32[128,128]{1,0:T(8,128)}, u32[]{:S(2)}) copy-start(f32[128,128]{1,0:T(8,128)} %constant.23.clone.sign) | copy-start | bytes 196612
  10.6 0.8 %copy-start.10 = (bf16[256,128]{1,0:T(8,128)(2,1)S(1)}, bf16[256,128]{1,0:T(8,128)(2,1)}, u32[]{:S(2)}) copy-start(bf16[256,128]{1,0:T(8,128)(2,1)} %constant.17.clone.a_low) | copy-start | bytes 196612
  11.4 0.8 %copy-start.11 = (f32[4,16,128]{2,1,0:T(8,128)S(1)}, f32[4,16,128]{2,1,0:T(8,128)}, u32[]{:S(2)}) copy-start(f32[4,16,128]{2,1,0:T(8,128)} %constant.19.clone.edges) | copy-start | bytes 98308

commit v2 on v1

v2 whole, which is shorter than its diff:
```python
import functools

import jax
import jax.numpy as jnp
import numpy as np
from jax import lax
from jax.experimental import pallas as pl
from jax.experimental.pallas import tpu as pltpu
from jax.sharding import PartitionSpec as P

MESH = pl.DeviceIdType.MESH
F32, BF16 = jnp.float32, jnp.bfloat16

CHANNELS = 4096
TOK = 128
CTX = 128
TEN = 4
FREQS = 2 * TOK * CTX
LOCAL = CHANNELS // TEN
OWN = LOCAL // CTX
PARTS = 1
PC = OWN // PARTS
HALF = CTX // 2
LOW = 8
HIGH = CTX // LOW
EPSILON = 1e-06


def tables():
    f = np.concatenate([np.arange(0, CTX, 2), np.arange(1, CTX, 2)]).astype(np.float64)
    a = np.arange(CTX, dtype=np.float64)
    first = 2 * np.pi * f[:, None] * a[None, :] / (2 * CTX)
    twist = 2 * np.pi * f[:, None] * a[None, :] / FREQS
    weight = np.where(f == 0, 1.0, 2.0)[:, None] / FREQS
    edge = 2 * np.pi * CTX * a / FREQS
    turn = np.stack([np.cos(twist), np.sin(twist), np.cos(twist) * weight, np.sin(twist) * weight])
    edges = np.stack([np.cos(edge), np.sin(edge), np.cos(edge) / FREQS, np.sin(edge) / FREQS])
    edges = np.repeat(edges[:, None, :], 16, axis=1)
    second = 2 * np.pi * a[:, None] * a[None, :] / TOK
    cos, sin = np.cos(second), np.sin(second)
    forward_a = np.concatenate([np.cos(first), -np.sin(first)], axis=0)
    forward_j = np.block([[cos, -sin], [sin, cos]])
    inverse_j = np.block([[cos, sin], [-sin, cos]])
    sign = np.repeat(np.where(a % 2 == 0, 1.0, -1.0)[:, None], TOK, axis=1)
    square = np.concatenate([forward_j, inverse_j, forward_a.T], axis=0)
    narrow = np.concatenate([turn.reshape(-1, TOK), edges.reshape(-1, TOK), sign, forward_a], axis=0)
    return square.astype(np.float32), narrow.astype(np.float32)


def split(value):
    high = value.astype(BF16)
    return high, (value - high.astype(F32)).astype(BF16)


def dot(left, right):
    return jnp.dot(left, right, preferred_element_type=F32)


def three_products(value, pair):
    rows = value.shape[0]
    high, low = split(value)
    both = dot(jnp.concatenate([high, low], axis=0), pair[0])
    return both[:rows] + both[rows:] + dot(high, pair[1])


def reversed_index(position):
    flipped = 0
    for place in range(7):
        flipped = flipped + ((position >> place) & 1) * (1 << (6 - place))
    return flipped


def mixer(
    query_hbm, key_hbm, value_hbm, spectrum_hbm, square_hbm, narrow_hbm, gain_hbm,
    gated, scale, gain,
    query, key, value, spectrum, square, narrow, load_sem, a_fwd, a_low, j_fwd, j_inv, a_inv,
    sending, arrived, answer, result, query_t, pieces, response, transformed, squares,
    send_sem, recv_sem, back_send, back_recv, filt_send, filt_recv, hand_sem, sq_send, sq_recv, own_sem, ready,
):
    me = lax.axis_index("context")
    mine = lax.axis_index("tensor")
    my_high, my_low = me // LOW, me % LOW

    def device(high, low):
        return (my_high ^ high) * LOW + (my_low ^ low)

    loads = [
        pltpu.make_async_copy(source, target, load_sem.at[number])
        for number, (source, target) in enumerate(
            [
                (key_hbm, key),
                (value_hbm, value),
                (spectrum_hbm, spectrum),
                (query_hbm, query),
                (square_hbm, square),
                (narrow_hbm, narrow),
                (gain_hbm, gain),
            ]
        )
    ]
    for load in loads:
        load.start()
    turn = [narrow.at[pl.ds(TOK * k, TOK)] for k in range(4)]
    edges = [narrow.at[pl.ds(4 * TOK + 16 * k, 16)] for k in range(4)]
    sign = narrow.at[pl.ds(4 * TOK + 64, TOK)]

    barrier = pltpu.get_barrier_semaphore()
    for high in range(HIGH - 1, 0, -1):
        pl.semaphore_signal(barrier, inc=1, device_id=(device(high, 0), mine), device_id_type=MESH)
    for step in (1, 3):
        pl.semaphore_signal(barrier, inc=1, device_id=(me, mine ^ step), device_id_type=MESH)
    for low in range(LOW - 1, 0, -1):
        pl.semaphore_signal(barrier, inc=1, device_id=(device(0, low), mine), device_id_type=MESH)

    loads[0].wait()
    loads[1].wait()
    for block in range(LOCAL // 128):
        columns = pl.ds(block * 128, 128)
        driven = key[:, columns].astype(F32) * value[:, columns].astype(F32)
        sending[columns, :] = driven.T

    pl.semaphore_wait(barrier, LOW - 1 + HIGH - 1 + 2)
    pl.semaphore_signal(ready.at[0], inc=1, device_id=(me, mine ^ 1), device_id_type=MESH)
    for low in range(LOW - 1, 0, -1):
        pl.semaphore_signal(ready.at[low], inc=1, device_id=(device(0, low), mine), device_id_type=MESH)

    def rows_of(start, count):
        return pl.ds(pl.multiple_of(start * count, count), count)

    def exchange(part, low, first):
        def step(high, carry):
            target = device(high, low)
            pltpu.make_async_remote_copy(
                src_ref=sending.at[rows_of(target * PARTS + part, PC)],
                dst_ref=arrived.at[part, rows_of(me, PC)],
                send_sem=send_sem.at[part],
                recv_sem=recv_sem.at[part],
                device_id=(target, mine),
                device_id_type=MESH,
            ).start()
            return carry

        lax.fori_loop(first, HIGH, step, 0)

    own = [
        pltpu.make_async_copy(
            sending.at[rows_of(me * PARTS + part, PC)], arrived.at[part, rows_of(me, PC)], own_sem.at[part]
        )
        for part in range(PARTS)
    ]
    for part in range(PARTS):
        own[part].start()
        for low in range(LOW):
            if low and not part:
                pl.semaphore_wait(ready.at[low], 1)
            exchange(part, low, 0 if low else 1)

    order = reversed_index(me)
    loads[2].wait()
    for kind in range(4):
        pieces[pl.ds(kind, LOCAL // 16, stride=4), :] = spectrum[kind // 2, kind % 2]

    def filter_copy(chip):
        return pltpu.make_async_remote_copy(
            src_ref=pieces.at[rows_of(chip, 4)],
            dst_ref=response.at[rows_of(order, 4)],
            send_sem=filt_send,
            recv_sem=filt_recv,
            device_id=(2 * chip, mine),
            device_id_type=MESH,
        )

    first_core = me % 2 == 0
    hand_on = pltpu.make_async_remote_copy(
        src_ref=response.at[pl.ds(0, 4 * HALF + 4)],
        dst_ref=response.at[pl.ds(0, 4 * HALF + 4)],
        send_sem=hand_sem,
        recv_sem=filt_recv,
        device_id=(me ^ 1, mine),
        device_id_type=MESH,
    )

    @pl.when(first_core)
    def _():
        def step(other, carry):
            filter_copy((me // 2) ^ other).start()
            return carry

        lax.fori_loop(1, CTX // 2, step, 0)
        local = pltpu.make_async_copy(
            pieces.at[rows_of(me // 2, 4)], response.at[rows_of(order, 4)], own_sem.at[PARTS]
        )
        local.start()
        local.wait()

    @pl.when(order == HALF)
    def _():
        def step(chip, carry):
            filter_copy(chip).start()
            return carry

        lax.fori_loop(0, CTX // 2, step, 0)

    loads[3].wait()
    for block in range(LOCAL // 128):
        columns = pl.ds(block * 128, 128)
        query_t[columns, :] = query[:, columns].astype(F32).T

    def wait_rows(ref, count, sem):
        pltpu.make_async_copy(ref.at[pl.ds(0, count)], ref.at[pl.ds(0, count)], sem).wait()

    loads[4].wait()
    loads[5].wait()
    loads[6].wait()
    for target, first in ((j_fwd, 0), (j_inv, 256)):
        target[0], target[1] = split(square[pl.ds(first, 256), :])
    a_inv[pl.ds(0, CTX), :], a_inv[pl.ds(CTX, CTX), :] = split(square[pl.ds(512, CTX), :])
    high, low = split(narrow[pl.ds(5 * TOK + 64, 256), :])
    a_fwd[:, :CTX], a_fwd[:, CTX:], a_low[...] = high, high, low
    for part in range(PARTS):
        own[part].wait()
        wait_rows(arrived.at[part], (CTX - 1) * PC, recv_sem.at[part])

        if part == 0:

            @pl.when(first_core)
            def _():
                wait_rows(response, HALF * 4, filt_recv)
                hand_on.start()

        block = arrived[part].reshape(CTX // 2, 2 * PC, TOK)
        folded = jnp.sum(block, axis=0)
        edge = folded[:PC] - folded[PC:]
        edge = jnp.concatenate([edge, jnp.zeros((16 - PC, TOK), F32)], axis=0)
        edge = jnp.concatenate([edge * edges[0][...], -edge * edges[1][...]], axis=1)
        edge = three_products(edge, j_fwd)

        for pair in range(PC // 2):
            high, low = split(
                jnp.concatenate(
                    [arrived[part, pl.ds(2 * pair + k, CTX, stride=PC), :] for k in (0, 1)], axis=1
                )
            )
            freq = dot(a_fwd[...], jnp.concatenate([high, low], axis=0)) + dot(a_low[...], high)
            rows = []
            for k in (0, 1):
                y_re, y_im = freq[:CTX, k * TOK : (k + 1) * TOK], freq[CTX:, k * TOK : (k + 1) * TOK]
                rows.append(
                    jnp.concatenate(
                        [y_re * turn[0][...] + y_im * turn[1][...], y_im * turn[0][...] - y_re * turn[1][...]],
                        axis=1,
                    )
                )
            transformed[pair] = three_products(jnp.concatenate(rows, axis=0), j_fwd)

        if part == 0:

            @pl.when(jnp.logical_not(first_core))
            def _():
                wait_rows(response, (HALF + 1) * 4, filt_recv)

        h_re = jnp.concatenate([response[pl.ds(kind, HALF, stride=4), :] for kind in (0, 1)], axis=0)
        h_im = jnp.concatenate([response[pl.ds(kind, HALF, stride=4), :] for kind in (2, 3)], axis=0)
        e_re, e_im = response[pl.ds(4 * HALF, 1), :], response[pl.ds(4 * HALF + 2, 1), :]
        z_re, z_im = edge[:, :TOK], edge[:, TOK:]
        edge = jnp.concatenate([z_re * e_re - z_im * e_im, z_re * e_im + z_im * e_re], axis=1)
        edge = three_products(edge, j_inv)
        edge = edge[:, :TOK] * edges[2][...] - edge[:, TOK:] * edges[3][...]

        for pair in range(PC // 2):
            rows = []
            for k in (0, 1):
                z_re = transformed[pair, pl.ds(k * CTX, CTX), pl.ds(0, TOK)]
                z_im = transformed[pair, pl.ds(k * CTX, CTX), pl.ds(TOK, TOK)]
                rows.append(jnp.concatenate([z_re * h_re - z_im * h_im, z_re * h_im + z_im * h_re], axis=1))
            back = three_products(jnp.concatenate(rows, axis=0), j_inv)
            columns = []
            for k in (0, 1):
                u_re, u_im = back[k * CTX : (k + 1) * CTX, :TOK], back[k * CTX : (k + 1) * CTX, TOK:]
                columns.append(
                    jnp.concatenate(
                        [u_re * turn[2][...] - u_im * turn[3][...], u_im * turn[2][...] + u_re * turn[3][...]],
                        axis=0,
                    )
                )
            high, low = split(jnp.concatenate(columns, axis=1))
            both = dot(a_inv[...], high)
            back = both[:CTX] + both[CTX:] + dot(a_inv[pl.ds(0, CTX), :], low)
            for k in (0, 1):
                channel = 2 * pair + k
                answer[part, pl.ds(channel, CTX, stride=PC), :] = (
                    back[:, k * TOK : (k + 1) * TOK] + sign[...] * edge[channel : channel + 1]
                )

        def step(other, carry):
            target = (me + other) % CTX
            pltpu.make_async_remote_copy(
                src_ref=answer.at[part, rows_of(target, PC)],
                dst_ref=result.at[rows_of(me * PARTS + part, PC)],
                send_sem=back_send,
                recv_sem=back_recv,
                device_id=(target, mine),
                device_id_type=MESH,
            ).start()
            return carry

        lax.fori_loop(1, CTX, step, 0)
        local = pltpu.make_async_copy(
            answer.at[part, rows_of(me, PC)], result.at[rows_of(me * PARTS + part, PC)], own_sem.at[part]
        )
        local.start()
        local.wait()

    wait_rows(result, (CTX - 1) * OWN, back_recv)
    total = jnp.zeros((8, TOK), F32)
    for block in range(LOCAL // 128):
        rows = pl.ds(block * 128, 128)
        mix = query_t[rows, :] * result[rows, :]
        gated[rows, :] = mix
        total = total + jnp.sum((mix * mix).reshape(16, 8, TOK), axis=0)
    squares[mine] = jnp.broadcast_to(jnp.sum(total, axis=0, keepdims=True), (8, TOK))
    copies = [
        pltpu.make_async_remote_copy(
            src_ref=squares.at[mine],
            dst_ref=squares.at[mine],
            send_sem=sq_send.at[step],
            recv_sem=sq_recv.at[step],
            device_id=(me, mine ^ step),
            device_id_type=MESH,
        )
        for step in range(1, TEN)
    ]
    pl.semaphore_wait(ready.at[0], 1)
    for copy in copies:
        copy.start()
    for part in range(PARTS):
        wait_rows(sending, (CTX - 1) * PC, send_sem.at[part])
    wait_rows(sending, (CTX - 1) * OWN, back_send)

    @pl.when(first_core)
    def _():
        wait_rows(sending, (CTX // 2 - 1) * 4, filt_send)
        hand_on.wait_send()

    @pl.when(order == HALF)
    def _():
        wait_rows(sending, CTX // 2 * 4, filt_send)

    for copy in copies:
        copy.wait()
    mean = (squares[0] + squares[1] + squares[2] + squares[3]) / CHANNELS
    scale[...] = lax.rsqrt(mean + EPSILON)


def finish(mixed, scale, gain, gated_hbm, normed_hbm, gated, normed, sems):
    column = scale[...].T[:, 0:1]
    copies = []
    blocks = 4
    wide = LOCAL // blocks
    for block in range(blocks):
        columns = pl.ds(block * wide, wide)
        value = mixed[columns, :].T
        gated[:, columns] = value
        normed[:, columns] = (value * column * gain[columns].astype(F32)[None, :]).astype(BF16)
        for number, (source, target) in enumerate(((gated, gated_hbm), (normed, normed_hbm))):
            copies.append(
                pltpu.make_async_copy(source.at[:, columns], target.at[:, columns], sems.at[2 * block + number])
            )
            copies[-1].start()
    for copy in copies:
        copy.wait()


def on_device(query_gate, key_branch, value_branch, filter_spectrum, norm_gain):
    vmem = pl.BlockSpec(memory_space=pltpu.VMEM)
    constants = [jnp.asarray(table) for table in tables()]
    mixed, scale, gain = pl.pallas_call(
        mixer,
        out_shape=(
            pltpu.VMEM((LOCAL, TOK), F32),
            pltpu.VMEM((8, TOK), F32),
            pltpu.VMEM((LOCAL,), BF16),
        ),
        in_specs=[pl.BlockSpec(memory_space=pl.ANY)] * 7,
        out_specs=(vmem,) * 3,
        scratch_shapes=[
            pltpu.VMEM((TOK, LOCAL), BF16),
            pltpu.VMEM((TOK, LOCAL), BF16),
            pltpu.VMEM((TOK, LOCAL), BF16),
            pltpu.VMEM((2, 2, LOCAL // 16, TOK), F32),
            pltpu.VMEM(constants[0].shape, F32),
            pltpu.VMEM(constants[1].shape, F32),
            pltpu.SemaphoreType.DMA((7,)),
            pltpu.VMEM((256, 256), BF16),
            pltpu.VMEM((256, CTX), BF16),
            pltpu.VMEM((2, 256, 256), BF16),
            pltpu.VMEM((2, 256, 256), BF16),
            pltpu.VMEM((256, 256), BF16),
            pltpu.VMEM((LOCAL, TOK), F32),
            pltpu.VMEM((PARTS, CTX * PC, TOK), F32),
            pltpu.VMEM((PARTS, CTX * PC, TOK), F32),
            pltpu.VMEM((LOCAL, TOK), F32),
            pltpu.VMEM((LOCAL, TOK), F32),
            pltpu.VMEM((LOCAL // 16 * 4, TOK), F32),
            pltpu.VMEM(((HALF + 2) * 4, TOK), F32),
            pltpu.VMEM((PC // 2, 2 * CTX, 2 * TOK), F32),
            pltpu.VMEM((TEN, 8, TOK), F32),
            pltpu.SemaphoreType.DMA((PARTS,)),
            pltpu.SemaphoreType.DMA((PARTS,)),
            pltpu.SemaphoreType.DMA,
            pltpu.SemaphoreType.DMA,
            pltpu.SemaphoreType.DMA,
            pltpu.SemaphoreType.DMA,
            pltpu.SemaphoreType.DMA,
            pltpu.SemaphoreType.DMA((TEN,)),
            pltpu.SemaphoreType.DMA((TEN,)),
            pltpu.SemaphoreType.DMA((PARTS + 1,)),
            pltpu.SemaphoreType.REGULAR((LOW,)),
        ],
        compiler_params=pltpu.CompilerParams(
            collective_id=0, has_side_effects=True, vmem_limit_bytes=60 << 20
        ),
    )(query_gate, key_branch, value_branch, filter_spectrum.reshape(2, 2, -1, TOK), *constants, norm_gain)
    return pl.pallas_call(
        finish,
        out_shape=(
            jax.ShapeDtypeStruct((TOK, LOCAL), F32),
            jax.ShapeDtypeStruct((TOK, LOCAL), BF16),
        ),
        in_specs=[vmem] * 3,
        out_specs=(pl.BlockSpec(memory_space=pl.ANY),) * 2,
        scratch_shapes=[
            pltpu.VMEM((TOK, LOCAL), F32),
            pltpu.VMEM((TOK, LOCAL), BF16),
            pltpu.SemaphoreType.DMA((8,)),
        ],
        compiler_params=pltpu.CompilerParams(vmem_limit_bytes=16 << 20),
    )(mixed, scale, gain)


def solution(mesh):
    placed = (
        P("context", "tensor"),
        P("context", "tensor"),
        P("context", "tensor"),
        P("context", None, None, "tensor", None),
        P("tensor"),
    )
    return jax.shard_map(
        on_device,
        mesh=mesh,
        in_specs=placed,
        out_specs=(P("context", "tensor"), P("context", "tensor")),
        check_vma=False,
    )
```

time: 73.9 us -> 56.7 us (0.77)
  the two profiles are of different devices: /device:TPU:1 before, /device:TPU:56 now
where the time goes in v2:
time: 56.7 us; the launch traced here: 56.6 us
  Pallas kernels  56 us (99%)
  between operations  0.64 us (1%)
    pallas_call x1, Pallas kernels, on_device(): pl.pallas_call(mixer, out_shape=(pltpu.VMEM((LOCAL, TOK), F32), pltpu.VME...  54.8 us
    pallas_call x1, Pallas kernels, on_device(): pl.pallas_call(finish, out_shape=(jax.ShapeDtypeStruct((TOK, LOCAL), F32)...  1.16 us

profile of v2, /device:TPU:56, one launch (start us, length us, event | category | flops | bytes accessed | tf_op | source)
XLA Modules:
  0.0 56.6 jit_solution(11940981690133615273)
XLA Ops:
  0.6 54.8 %shard_map.86 = (f32[1024,128]{1,0:T(8,128)S(1)}, f32[8,128]{1,0:T(8,128)S(1)}, bf16[1024]{0:T(1024)(128)(2,1)S(1)}) custom-call(bf16[128,1024]{1,0:T(8,128)(2,1)} %query_hbm.1, bf16[128,1024]{1,0:T(8,128)(2,1)} %key_hbm.1, bf16[128,1024]{1,0:T(8,128)(2,1)} %value_hbm.1, f32[2,2,64,128]{3,2,1,0:T(8,128)} %bitcast.1, f32[640,256]{1,0:T(8,128)} %constant.4.clone.square_hbm, ...), custom_call_target="tpu_custom_call" | custom-call | tf_op jit(solution)/shard_map/pallas_call | solution.py:377
  55.5 1.2 %shard_map.87 = (f32[128,1024]{1,0:T(8,128)}, bf16[128,1024]{1,0:T(8,128)(2,1)}) custom-call(f32[1024,128]{1,0:T(8,128)S(1)} %get-tuple-element.5.mixed, f32[8,128]{1,0:T(8,128)S(1)} %get-tuple-element.6.scale, bf16[1024]{0:T(1024)(128)(2,1)S(1)} %get-tuple-element.7.gain), custom_call_target="tpu_custom_call" | custom-call | tf_op jit(solution)/shard_map/pallas_call | solution.py:424

commit v3 on v2

v3 whole, which is shorter than its diff:
```python
import functools

import jax
import jax.numpy as jnp
import numpy as np
from jax import lax
from jax.experimental import pallas as pl
from jax.experimental.pallas import tpu as pltpu
from jax.sharding import PartitionSpec as P

MESH = pl.DeviceIdType.MESH
F32, BF16 = jnp.float32, jnp.bfloat16

CHANNELS = 4096
TOK = 128
CTX = 128
TEN = 4
FREQS = 2 * TOK * CTX
LOCAL = CHANNELS // TEN
OWN = LOCAL // CTX
PARTS = 2
PC = OWN // PARTS
CHIPS = CTX // 2
PACK = 2 * PC
HALF = CTX // 2
EPSILON = 1e-06


def tables():
    f = np.concatenate([np.arange(0, CTX, 2), np.arange(1, CTX, 2)]).astype(np.float64)
    a = np.arange(CTX, dtype=np.float64)
    first = 2 * np.pi * f[:, None] * a[None, :] / (2 * CTX)
    twist = 2 * np.pi * f[:, None] * a[None, :] / FREQS
    weight = np.where(f == 0, 1.0, 2.0)[:, None] / FREQS
    edge = 2 * np.pi * CTX * a / FREQS
    turn = np.stack([np.cos(twist), np.sin(twist), np.cos(twist) * weight, np.sin(twist) * weight])
    edges = np.stack([np.cos(edge), np.sin(edge), np.cos(edge) / FREQS, np.sin(edge) / FREQS])
    edges = np.repeat(edges[:, None, :], 16, axis=1)
    second = 2 * np.pi * a[:, None] * a[None, :] / TOK
    cos, sin = np.cos(second), np.sin(second)
    forward_j = np.block([[cos, -sin], [sin, cos]])
    inverse_j = np.block([[cos, sin], [-sin, cos]])
    first = [np.concatenate([first[:, core::2], first[:, 1 - core :: 2]], axis=1) for core in (0, 1)]
    forward_a = [np.concatenate([np.cos(angle), -np.sin(angle)], axis=0) for angle in first]
    square = np.concatenate([forward_j, inverse_j, forward_a[0].T, forward_a[1].T], axis=0)
    narrow = np.concatenate([turn.reshape(-1, TOK), edges.reshape(-1, TOK), *forward_a], axis=0)
    return square.astype(np.float32), narrow.astype(np.float32)


def split(value):
    high = value.astype(BF16)
    return high, (value - high.astype(F32)).astype(BF16)


def dot(left, right):
    return jnp.dot(left, right, preferred_element_type=F32)


def three_products(value, pair):
    rows = value.shape[0]
    high, low = split(value)
    both = dot(jnp.concatenate([high, low], axis=0), pair[0])
    return both[:rows] + both[rows:] + dot(high, pair[1])


def reversed_index(position):
    flipped = 0
    for place in range(7):
        flipped = flipped + ((position >> place) & 1) * (1 << (6 - place))
    return flipped


def mixer(
    query_hbm, key_hbm, value_hbm, spectrum_hbm, square_hbm, narrow_hbm, gain_hbm,
    gated, scale, gain,
    query, key, value, spectrum, square, narrow, load_sem, a_fwd, a_low, j_fwd, j_inv, a_inv,
    sending, arrived, handed, answer, back_arrived, back_handed, result, query_t, pieces, response, transformed, squares,
    out_sem, in_sem, filt_send, filt_recv, hand_sem, sq_send, sq_recv, own_sem, ready,
):
    me = lax.axis_index("context")
    mine = lax.axis_index("tensor")
    chip, core = me // 2, me % 2

    j_rows, n_rows = 512, 4 * TOK + 64
    loads = [
        pltpu.make_async_copy(source, target, load_sem.at[number])
        for number, (source, target) in enumerate(
            [
                (key_hbm, key),
                (value_hbm, value),
                (spectrum_hbm, spectrum),
                (query_hbm, query),
                (square_hbm.at[pl.ds(0, j_rows)], square.at[pl.ds(0, j_rows)]),
                (square_hbm.at[pl.ds(j_rows + CTX * core, CTX)], square.at[pl.ds(j_rows, CTX)]),
                (narrow_hbm.at[pl.ds(0, n_rows)], narrow.at[pl.ds(0, n_rows)]),
                (narrow_hbm.at[pl.ds(n_rows + 256 * core, 256)], narrow.at[pl.ds(n_rows, 256)]),
                (gain_hbm, gain),
            ]
        )
    ]
    for load in loads:
        load.start()
    turn = [narrow.at[pl.ds(TOK * k, TOK)] for k in range(4)]
    edges = [narrow.at[pl.ds(4 * TOK + 16 * k, 16)] for k in range(4)]

    barrier = pltpu.get_barrier_semaphore()
    for step in (1, 3):
        pl.semaphore_signal(barrier, inc=1, device_id=(me, mine ^ step), device_id_type=MESH)

    def greet(other, carry):
        target = chip ^ (CHIPS - other)
        pl.semaphore_signal(barrier, inc=1, device_id=(2 * target + core, mine), device_id_type=MESH)
        return carry

    lax.fori_loop(1, CHIPS, greet, 0)
    pl.semaphore_signal(barrier, inc=1, device_id=(me ^ 1, mine), device_id_type=MESH)

    loads[0].wait()
    loads[1].wait()
    for block in range(LOCAL // 128):
        columns = pl.ds(block * 128, 128)
        driven = key[:, columns].astype(F32) * value[:, columns].astype(F32)
        driven = driven.T.reshape(8, 2, OWN, TOK)
        same = jnp.where(core == 0, driven[:, 0], driven[:, 1])
        other = jnp.where(core == 0, driven[:, 1], driven[:, 0])
        for part in range(PARTS):
            few = slice(part * PC, (part + 1) * PC)
            sending[part, pl.ds(block * 8 * PACK, 8 * PACK), :] = jnp.concatenate(
                [same[:, few], other[:, few]], axis=1
            ).reshape(8 * PACK, TOK)

    order = reversed_index(me)
    first_core = core == 0
    loads[2].wait()
    for kind in range(4):
        pieces[pl.ds(kind, LOCAL // 16, stride=4), :] = spectrum[kind // 2, kind % 2]

    pl.semaphore_wait(barrier, CHIPS - 1 + 3)
    pl.semaphore_signal(ready.at[0], inc=1, device_id=(me, mine ^ 1), device_id_type=MESH)

    @pl.when(core == 0)
    def _():
        pl.semaphore_signal(ready.at[1], inc=1, device_id=(me ^ 1, mine), device_id_type=MESH)


    def rows_of(start, count):
        return pl.ds(pl.multiple_of(start * count, count), count)

    def exchange(part, source, landing, kind):
        def step(other, carry):
            target = chip ^ (CHIPS - other) if kind == 0 else (chip + other) % CHIPS
            pltpu.make_async_remote_copy(
                src_ref=source.at[part, rows_of(target, PACK)],
                dst_ref=landing.at[part, chip],
                send_sem=out_sem.at[kind, part],
                recv_sem=in_sem.at[kind, part],
                device_id=(2 * target + core, mine),
                device_id_type=MESH,
            ).start()
            return carry

        lax.fori_loop(1, CHIPS, step, 0)
        own = pltpu.make_async_copy(
            source.at[part, rows_of(chip, PACK)], landing.at[part, chip], own_sem.at[kind // 2 * PARTS + part]
        )
        own.start()
        return own

    def hand(part, landing, target, kind):
        share = pl.ds(PC, PC)
        return pltpu.make_async_remote_copy(
            src_ref=landing.at[part, :, share],
            dst_ref=target.at[part, :, share],
            send_sem=out_sem.at[kind, part],
            recv_sem=in_sem.at[kind, part],
            device_id=(me ^ 1, mine),
            device_id_type=MESH,
        )

    def wait_blocks(ref, count, sem):
        pltpu.make_async_copy(ref.at[pl.ds(0, count)], ref.at[pl.ds(0, count)], sem).wait()

    def filter_copy(target):
        return pltpu.make_async_remote_copy(
            src_ref=pieces.at[rows_of(target, 4)],
            dst_ref=response.at[rows_of(order, 4)],
            send_sem=filt_send,
            recv_sem=filt_recv,
            device_id=(2 * target, mine),
            device_id_type=MESH,
        )

    hand_on = pltpu.make_async_remote_copy(
        src_ref=response.at[pl.ds(0, 4 * HALF + 4)],
        dst_ref=response.at[pl.ds(0, 4 * HALF + 4)],
        send_sem=hand_sem,
        recv_sem=filt_recv,
        device_id=(me ^ 1, mine),
        device_id_type=MESH,
    )

    @pl.when(first_core)
    def _():
        def step(other, carry):
            filter_copy((chip + other) % CHIPS).start()
            return carry

        lax.fori_loop(1, CHIPS, step, 0)
        local = pltpu.make_async_copy(
            pieces.at[rows_of(chip, 4)], response.at[rows_of(order, 4)], own_sem.at[2 * PARTS]
        )
        local.start()
        local.wait()

    @pl.when(jnp.logical_not(first_core))
    def _():
        pl.semaphore_wait(ready.at[1], 1)

    @pl.when(order == HALF)
    def _():
        def step(target, carry):
            filter_copy(target).start()
            return carry

        lax.fori_loop(0, CHIPS, step, 0)

    forward = [exchange(part, sending, arrived, 0) for part in range(PARTS)]
    hands = [hand(part, arrived, handed, 1) for part in range(PARTS)]

    loads[3].wait()
    for block in range(LOCAL // 128):
        columns = pl.ds(block * 128, 128)
        query_t[columns, :] = query[:, columns].astype(F32).T

    for load in loads[4:]:
        load.wait()
    for target, first in ((j_fwd, 0), (j_inv, 256)):
        target[0], target[1] = split(square[pl.ds(first, 256), :])
    a_inv[pl.ds(0, CTX), :], a_inv[pl.ds(CTX, CTX), :] = split(square[pl.ds(512, CTX), :])
    high, low = split(narrow[pl.ds(n_rows, 256), :])
    a_fwd[:, :CTX], a_fwd[:, CTX:], a_low[...] = high, high, low
    parity = jnp.where(core == 0, 1.0, -1.0)

    backward = []
    for part in range(PARTS):
        forward[part].wait()
        wait_blocks(arrived.at[part], CHIPS - 1, in_sem.at[0, part])
        hands[part].start()
        if part == 0:

            @pl.when(first_core)
            def _():
                wait_blocks(response, HALF * 4, filt_recv)
                hand_on.start()

        hands[part].wait_recv()

        edge = jnp.sum(arrived[part, :, pl.ds(0, PC), :], axis=0) - jnp.sum(handed[part, :, pl.ds(PC, PC), :], axis=0)
        edge = jnp.concatenate([edge * parity, jnp.zeros((16 - PC, TOK), F32)], axis=0)
        edge = jnp.concatenate([edge * edges[0][...], -edge * edges[1][...]], axis=1)
        edge = three_products(edge, j_fwd)

        near = arrived.at[part].reshape(CHIPS * PACK, TOK)
        far = handed.at[part].reshape(CHIPS * PACK, TOK)
        for pair in range(PC // 2):
            columns = []
            for k in (0, 1):
                channel = 2 * pair + k
                columns.append(
                    jnp.concatenate(
                        [
                            near[pl.ds(channel, CHIPS, stride=PACK), :],
                            far[pl.ds(PC + channel, CHIPS, stride=PACK), :],
                        ],
                        axis=0,
                    )
                )
            high, low = split(jnp.concatenate(columns, axis=1))
            freq = dot(a_fwd[...], jnp.concatenate([high, low], axis=0)) + dot(a_low[...], high)
            rows = []
            for k in (0, 1):
                y_re, y_im = freq[:CTX, k * TOK : (k + 1) * TOK], freq[CTX:, k * TOK : (k + 1) * TOK]
                rows.append(
                    jnp.concatenate(
                        [y_re * turn[0][...] + y_im * turn[1][...], y_im * turn[0][...] - y_re * turn[1][...]],
                        axis=1,
                    )
                )
            transformed[pair] = three_products(jnp.concatenate(rows, axis=0), j_fwd)

        if part == 0:

            @pl.when(jnp.logical_not(first_core))
            def _():
                wait_blocks(response, (HALF + 1) * 4, filt_recv)

        h_re = jnp.concatenate([response[pl.ds(kind, HALF, stride=4), :] for kind in (0, 1)], axis=0)
        h_im = jnp.concatenate([response[pl.ds(kind, HALF, stride=4), :] for kind in (2, 3)], axis=0)
        e_re, e_im = response[pl.ds(4 * HALF, 1), :], response[pl.ds(4 * HALF + 2, 1), :]
        z_re, z_im = edge[:, :TOK], edge[:, TOK:]
        edge = jnp.concatenate([z_re * e_re - z_im * e_im, z_re * e_im + z_im * e_re], axis=1)
        edge = three_products(edge, j_inv)
        edge = (edge[:, :TOK] * edges[2][...] - edge[:, TOK:] * edges[3][...]) * parity

        for pair in range(PC // 2):
            rows = []
            for k in (0, 1):
                z_re = transformed[pair, pl.ds(k * CTX, CTX), pl.ds(0, TOK)]
                z_im = transformed[pair, pl.ds(k * CTX, CTX), pl.ds(TOK, TOK)]
                rows.append(jnp.concatenate([z_re * h_re - z_im * h_im, z_re * h_im + z_im * h_re], axis=1))
            back = three_products(jnp.concatenate(rows, axis=0), j_inv)
            columns = []
            for k in (0, 1):
                u_re, u_im = back[k * CTX : (k + 1) * CTX, :TOK], back[k * CTX : (k + 1) * CTX, TOK:]
                columns.append(
                    jnp.concatenate(
                        [u_re * turn[2][...] - u_im * turn[3][...], u_im * turn[2][...] + u_re * turn[3][...]],
                        axis=0,
                    )
                )
            high, low = split(jnp.concatenate(columns, axis=1))
            both = dot(a_inv[...], high)
            back = both[:CTX] + both[CTX:] + dot(a_inv[pl.ds(0, CTX), :], low)
            for k in (0, 1):
                channel = 2 * pair + k
                row, wide = edge[channel : channel + 1], slice(k * TOK, (k + 1) * TOK)
                answer[part, pl.ds(channel, CHIPS, stride=PACK), :] = back[:CHIPS, wide] + row
                answer[part, pl.ds(PC + channel, CHIPS, stride=PACK), :] = back[CHIPS:, wide] - row

        backward.append(exchange(part, answer, back_arrived, 2))

    back_hands = [hand(part, back_arrived, back_handed, 3) for part in range(PARTS)]
    for part in range(PARTS):
        backward[part].wait()
        wait_blocks(back_arrived.at[part], CHIPS - 1, in_sem.at[2, part])
        back_hands[part].start()
    for part in range(PARTS):
        back_hands[part].wait_recv()

    total = jnp.zeros((8, TOK), F32)
    for block in range(LOCAL // 128):
        rows, chips = pl.ds(block * 128, 128), pl.ds(block * 8, 8)
        near = jnp.concatenate([back_arrived[part, chips, pl.ds(0, PC), :] for part in range(PARTS)], axis=1)
        far = jnp.concatenate([back_handed[part, chips, pl.ds(PC, PC), :] for part in range(PARTS)], axis=1)
        convolved = jnp.stack([jnp.where(core == 0, near, far), jnp.where(core == 0, far, near)], axis=1)
        mix = query_t[rows, :] * convolved.reshape(128, TOK)
        result[rows, :] = mix
        total = total + jnp.sum((mix * mix).reshape(16, 8, TOK), axis=0)
    squares[mine] = jnp.broadcast_to(jnp.sum(total, axis=0, keepdims=True), (8, TOK))
    copies = [
        pltpu.make_async_remote_copy(
            src_ref=squares.at[mine],
            dst_ref=squares.at[mine],
            send_sem=sq_send.at[step],
            recv_sem=sq_recv.at[step],
            device_id=(me, mine ^ step),
            device_id_type=MESH,
        )
        for step in (2, 1, 3)
    ]
    pl.semaphore_wait(ready.at[0], 1)
    for copy in copies:
        copy.start()
    for block in range(LOCAL // 128):
        rows = pl.ds(block * 128, 128)
        gated[:, rows] = result[rows, :].T
    for part in range(PARTS):
        wait_blocks(arrived.at[part], CHIPS - 1, out_sem.at[0, part])
        wait_blocks(arrived.at[part], CHIPS - 1, out_sem.at[2, part])
        hands[part].wait_send()
        back_hands[part].wait_send()

    @pl.when(first_core)
    def _():
        wait_blocks(pieces, (CHIPS - 1) * 4, filt_send)
        hand_on.wait_send()

    @pl.when(order == HALF)
    def _():
        wait_blocks(pieces, CHIPS * 4, filt_send)

    for copy in copies:
        copy.wait()
    mean = (squares[0] + squares[1] + squares[2] + squares[3]) / CHANNELS
    scale[...] = lax.rsqrt(mean + EPSILON)


def finish(gated, scale, gain, gated_hbm, normed_hbm, normed, sems):
    copies = [pltpu.make_async_copy(gated, gated_hbm, sems.at[0])]
    copies[0].start()
    column = scale[...].T[:, 0:1]
    blocks = 4
    wide = LOCAL // blocks
    for block in range(blocks):
        columns = pl.ds(block * wide, wide)
        normed[:, columns] = (gated[:, columns] * column * gain[columns].astype(F32)[None, :]).astype(BF16)
        copies.append(pltpu.make_async_copy(normed.at[:, columns], normed_hbm.at[:, columns], sems.at[block + 1]))
        copies[-1].start()
    for copy in copies:
        copy.wait()


def on_device(query_gate, key_branch, value_branch, filter_spectrum, norm_gain):
    vmem = pl.BlockSpec(memory_space=pltpu.VMEM)
    constants = [jnp.asarray(table) for table in tables()]
    mixed, scale, gain = pl.pallas_call(
        mixer,
        out_shape=(
            pltpu.VMEM((TOK, LOCAL), F32),
            pltpu.VMEM((8, TOK), F32),
            pltpu.VMEM((LOCAL,), BF16),
        ),
        in_specs=[pl.BlockSpec(memory_space=pl.ANY)] * 7,
        out_specs=(vmem,) * 3,
        scratch_shapes=[
            pltpu.VMEM((TOK, LOCAL), BF16),
            pltpu.VMEM((TOK, LOCAL), BF16),
            pltpu.VMEM((TOK, LOCAL), BF16),
            pltpu.VMEM((2, 2, LOCAL // 16, TOK), F32),
            pltpu.VMEM((512 + CTX, 256), F32),
            pltpu.VMEM((4 * TOK + 64 + 256, TOK), F32),
            pltpu.SemaphoreType.DMA((9,)),
            pltpu.VMEM((256, 256), BF16),
            pltpu.VMEM((256, CTX), BF16),
            pltpu.VMEM((2, 256, 256), BF16),
            pltpu.VMEM((2, 256, 256), BF16),
            pltpu.VMEM((256, 256), BF16),
            pltpu.VMEM((PARTS, CHIPS * PACK, TOK), F32),
            pltpu.VMEM((PARTS, CHIPS, PACK, TOK), F32),
            pltpu.VMEM((PARTS, CHIPS, PACK, TOK), F32),
            pltpu.VMEM((PARTS, CHIPS * PACK, TOK), F32),
            pltpu.VMEM((PARTS, CHIPS, PACK, TOK), F32),
            pltpu.VMEM((PARTS, CHIPS, PACK, TOK), F32),
            pltpu.VMEM((LOCAL, TOK), F32),
            pltpu.VMEM((LOCAL, TOK), F32),
            pltpu.VMEM((LOCAL // 16 * 4, TOK), F32),
            pltpu.VMEM(((HALF + 2) * 4, TOK), F32),
            pltpu.VMEM((PC // 2, 2 * CTX, 2 * TOK), F32),
            pltpu.VMEM((TEN, 8, TOK), F32),
            pltpu.SemaphoreType.DMA((4, PARTS)),
            pltpu.SemaphoreType.DMA((4, PARTS)),
            pltpu.SemaphoreType.DMA,
            pltpu.SemaphoreType.DMA,
            pltpu.SemaphoreType.DMA,
            pltpu.SemaphoreType.DMA((TEN,)),
            pltpu.SemaphoreType.DMA((TEN,)),
            pltpu.SemaphoreType.DMA((2 * PARTS + 1,)),
            pltpu.SemaphoreType.REGULAR((2,)),
        ],
        compiler_params=pltpu.CompilerParams(
            collective_id=0, has_side_effects=True, vmem_limit_bytes=60 << 20
        ),
    )(query_gate, key_branch, value_branch, filter_spectrum.reshape(2, 2, -1, TOK), *constants, norm_gain)
    return pl.pallas_call(
        finish,
        out_shape=(
            jax.ShapeDtypeStruct((TOK, LOCAL), F32),
            jax.ShapeDtypeStruct((TOK, LOCAL), BF16),
        ),
        in_specs=[vmem] * 3,
        out_specs=(pl.BlockSpec(memory_space=pl.ANY),) * 2,
        scratch_shapes=[
            pltpu.VMEM((TOK, LOCAL), BF16),
            pltpu.SemaphoreType.DMA((5,)),
        ],
        compiler_params=pltpu.CompilerParams(vmem_limit_bytes=16 << 20),
    )(mixed, scale, gain)


def solution(mesh):
    placed = (
        P("context", "tensor"),
        P("context", "tensor"),
        P("context", "tensor"),
        P("context", None, None, "tensor", None),
        P("tensor"),
    )
    return jax.shard_map(
        on_device,
        mesh=mesh,
        in_specs=placed,
        out_specs=(P("context", "tensor"), P("context", "tensor")),
        check_vma=False,
    )
```

time: 56.7 us -> 55.3 us (0.975)
  the two profiles are of different devices: /device:TPU:56 before, /device:TPU:1 now
where the time goes in v3:
time: 55.3 us; the launch traced here: 55.1 us
  Pallas kernels  54.5 us (99%)
  between operations  0.64 us (1%)
    pallas_call x1, Pallas kernels, on_device(): pl.pallas_call(mixer, out_shape=(pltpu.VMEM((TOK, LOCAL), F32), pltpu.VME...  53.6 us

profile of v3, /device:TPU:1, one launch (start us, length us, event | category | flops | bytes accessed | tf_op | source)
XLA Modules:
  0.0 55.1 jit_solution(3866367335415783230)
XLA Ops:
  0.6 53.6 %shard_map.86 = (f32[128,1024]{1,0:T(8,128)S(1)}, f32[8,128]{1,0:T(8,128)S(1)}, bf16[1024]{0:T(1024)(128)(2,1)S(1)}) custom-call(bf16[128,1024]{1,0:T(8,128)(2,1)} %query_hbm.1, bf16[128,1024]{1,0:T(8,128)(2,1)} %key_hbm.1, bf16[128,1024]{1,0:T(8,128)(2,1)} %value_hbm.1, f32[2,2,64,128]{3,2,1,0:T(8,128)} %bitcast.1, f32[768,256]{1,0:T(8,128)} %constant.4.clone.square_hbm, ...), custom_call_target="tpu_custom_call" | custom-call | tf_op jit(solution)/shard_map/pallas_call | solution.py:406
  54.2 0.9 %shard_map.87 = (f32[128,1024]{1,0:T(8,128)}, bf16[128,1024]{1,0:T(8,128)(2,1)}) custom-call(f32[128,1024]{1,0:T(8,128)S(1)} %get-tuple-element.5.gated, f32[8,128]{1,0:T(8,128)S(1)} %get-tuple-element.6.scale, bf16[1024]{0:T(1024)(128)(2,1)S(1)} %get-tuple-element.7.gain), custom_call_target="tpu_custom_call" | custom-call | tf_op jit(solution)/shard_map/pallas_call | solution.py:454
